TPU v7x, 32 devices: a whole 2x2x4 slice. The times are simulated.
32 devices in a mesh: dp: 8 (over y, x, core), tensor: 4 (over z).
Axes of the slice: x: 2, y: 2, z: 4, core: 2. Of those that a mesh axis runs over, the one named last changes fastest.
Arguments:
- inputs: bfloat16 [16384, 768], P('dp'), may hold values from -6 to 6
- gain1: float32 [768], replicated, may hold values from 0.1 to 1.9
- bias1: float32 [768], replicated, may hold values from -1 to 1
- w_qkv: bfloat16 [768, 3, 768], P(None, None, 'tensor'), may hold values from -0.3125 to 0.3125
- bias_q: float32 [768], P('tensor'), may hold values from -1.5 to 1.5
- bias_v: float32 [768], P('tensor'), may hold values from -1.5 to 1.5
- w_out: bfloat16 [768, 768], P('tensor'), may hold values from -1 to 1
- bias_out: float32 [768], replicated, may hold values from -1 to 1
- gain2: float32 [768], replicated, may hold values from 0.1 to 1.9
- bias2: float32 [768], replicated, may hold values from -1 to 1
- w_fc: bfloat16 [768, 3072], P(None, 'tensor'), may hold values from -0.21875 to 0.21875
- bias_fc: float32 [3072], P('tensor'), may hold values from -1.5 to 1.5
- w_proj: bfloat16 [3072, 768], P('tensor'), may hold values from -0.15625 to 0.15625
- bias_proj: float32 [768], replicated, may hold values from -2 to 2
- cotangent: bfloat16 [16384, 768], P('dp'), may hold values from -6 to 6
Outputs:
- output: bfloat16 [16384, 768], P('dp')
- d_inputs: bfloat16 [16384, 768], P('dp')
- d_gain1: float32 [768], replicated
- d_bias1: float32 [768], replicated
- d_w_qkv: float32 [768, 3, 768], P(None, None, 'tensor')
- d_bias_q: float32 [768], P('tensor')
- d_bias_v: float32 [768], P('tensor')
- d_w_out: float32 [768, 768], P('tensor')
- d_bias_out: float32 [768], replicated
- d_gain2: float32 [768], replicated
- d_bias2: float32 [768], replicated
- d_w_fc: float32 [768, 3072], P(None, 'tensor')
- d_bias_fc: float32 [3072], P('tensor')
- d_w_proj: float32 [3072, 768], P('tensor')
- d_bias_proj: float32 [768], replicated
All inputs are finite; a program needn't handle non-finite values.
Results may differ from a plain program's by a relative error of at most 0.02.
Values may be sent and summed in bfloat16 or wider, within the bound.
No kernel may reach another device: no remote copies, remote signals or barrier semaphores. Data moves between devices by JAX's collectives and lax.ppermute only.
A program may use at most 128 MiB of HBM per device.

v0:
```python
import jax
import jax.numpy as jnp
from jax import lax
from jax.experimental import pallas as pl
from jax.experimental.pallas import tpu as pltpu
from jax.sharding import PartitionSpec as P

HEAD = 64
LEN = 1024
BLOCK = 256
UNITS = 768
VMEM = 32 * 2**20
SMALL = pl.CostEstimate(flops=1, bytes_accessed=1, transcendentals=0)


LOW = jnp.bfloat16
WIDE = jnp.float32

NN = (((1,), (0,)), ((), ()))
NT = (((1,), (1,)), ((), ()))
TN = (((0,), (0,)), ((), ()))
TT = (((0,), (1,)), ((), ()))


def dot(left, right, dims=NN):
    return lax.dot_general(left, right, dims, preferred_element_type=WIDE)


def norm_parts(value):
    centre = value - jnp.mean(value, axis=-1, keepdims=True)
    rstd = lax.rsqrt(jnp.mean(centre * centre, axis=-1, keepdims=True) + 1e-05)
    return (centre * rstd, rstd)


def norm_back(normed, rstd, gain, grad):
    scaled = grad * gain
    inner = (
        scaled
        - jnp.mean(scaled, axis=-1, keepdims=True)
        - normed * jnp.mean(scaled * normed, axis=-1, keepdims=True)
    )
    return (rstd * inner, jnp.sum(grad * normed, axis=0), jnp.sum(grad, axis=0))


def causal(scores):
    keys = lax.broadcasted_iota(jnp.int32, scores.shape, 0)
    queries = lax.broadcasted_iota(jnp.int32, scores.shape, 1)
    return keys <= queries


def attend(q_ref, k_ref, v_ref, o_ref, lse_ref):
    query, values = q_ref[0, 0], v_ref[0, 0]
    keys = k_ref[0, 0].T
    for lo in range(0, LEN, BLOCK):
        hi = lo + BLOCK
        near = dot(keys[lo:hi], query[:, lo:hi])
        near = jnp.where(causal(near), near, -1e30)
        top = jnp.max(near, axis=0, keepdims=True)
        if lo:
            far = dot(keys[:lo], query[:, lo:hi])
            top = jnp.maximum(top, jnp.max(far, axis=0, keepdims=True))
        near = jnp.exp(near - top)
        total = jnp.sum(near, axis=0, keepdims=True)
        out = dot(values[:, lo:hi], near.astype(LOW))
        if lo:
            far = jnp.exp(far - top)
            total += jnp.sum(far, axis=0, keepdims=True)
            out += dot(values[:, :lo], far.astype(LOW))
        o_ref[0, :, lo:hi] = (out / total).astype(LOW)
        lse_ref[0, :, lo:hi] = top + jnp.log(total)


def attend_back(q_ref, k_ref, v_ref, o_ref, do_ref, lse_ref, *refs):
    out_ref, dq_ref = refs[-2:]
    query, keys_t, d_out = q_ref[0, 0], k_ref[0, 0], do_ref[0]
    keys, values = keys_t.T, v_ref[0, 0].T
    lse = lse_ref[0]
    delta = jnp.sum(d_out.astype(WIDE) * o_ref[0].astype(WIDE), axis=0, keepdims=True)

    def part(lo, hi, begin, end, mask):
        probs = jnp.exp(dot(keys[lo:hi], query[:, begin:end]) - lse[:, begin:end])
        if mask:
            probs = jnp.where(causal(probs), probs, 0.0)
        d_probs = dot(values[lo:hi], d_out[:, begin:end])
        d_scores = (probs * (d_probs - delta[:, begin:end])).astype(LOW)
        d_values = dot(d_out[:, begin:end], probs.astype(LOW), NT)
        d_keys = dot(query[:, begin:end], d_scores, NT)
        d_query = dot(keys_t[:, lo:hi], d_scores)
        if lo == 0:
            dq_ref[:, begin:end] = d_query
        else:
            dq_ref[:, begin:end] += d_query
        return d_keys, d_values

    for lo in range(0, LEN, BLOCK):
        hi = lo + BLOCK
        d_keys, d_values = part(lo, hi, lo, hi, True)
        if hi < LEN:
            more_keys, more_values = part(lo, hi, hi, LEN, False)
            d_keys += more_keys
            d_values += more_values
        out_ref[1, 0, :, lo:hi] = d_keys.astype(LOW)
        out_ref[2, 0, :, lo:hi] = d_values.astype(LOW)
    d_query = dq_ref[...].astype(LOW).astype(WIDE) * HEAD ** (-0.5)
    out_ref[0, 0] = d_query.astype(LOW)


ANY = pl.BlockSpec(memory_space=pl.ANY)


def kind(which):
    return pl.BlockSpec((1, 1, HEAD, LEN), lambda head: (which, head, 0, 0))


QKV = [kind(0), kind(1), kind(2)]
PER_HEAD = pl.BlockSpec((1, HEAD, LEN), lambda head: (head, 0, 0))
PER_ROW = pl.BlockSpec((1, 1, LEN), lambda head: (head, 0, 0))


def attention(qkv):
    heads = qkv.shape[1]
    return pl.pallas_call(
        attend,
        grid=(heads,),
        in_specs=QKV,
        out_specs=[PER_HEAD, PER_ROW],
        out_shape=[
            jax.ShapeDtypeStruct((heads, HEAD, LEN), LOW),
            jax.ShapeDtypeStruct((heads, 1, LEN), WIDE),
        ],
        compiler_params=pltpu.CompilerParams(vmem_limit_bytes=VMEM),
        cost_estimate=SMALL,
        name="attention",
    )(qkv, qkv, qkv)


def attention_back(qkv, out, d_out, lse, *earlier):
    heads = qkv.shape[1]
    return pl.pallas_call(
        attend_back,
        grid=(heads,),
        in_specs=QKV + [PER_HEAD, PER_HEAD, PER_ROW] + [ANY] * len(earlier),
        out_specs=pl.BlockSpec((3, 1, HEAD, LEN), lambda head: (0, head, 0, 0)),
        out_shape=jax.ShapeDtypeStruct((3, heads, HEAD, LEN), LOW),
        scratch_shapes=[pltpu.VMEM((HEAD, LEN), WIDE)],
        compiler_params=pltpu.CompilerParams(vmem_limit_bytes=VMEM),
        cost_estimate=SMALL,
        name="attention_back",
    )(qkv, qkv, qkv, out, d_out, lse, *earlier)


def bits(size, odd):
    above = [1 << b for b in range(1, size.bit_length() - 1)]
    return above if odd else above[::-1]


def exchanges(size):
    steps = [
        [(d, d ^ (odd if d & 1 else even)) for d in range(size)]
        for even, odd in zip(bits(size, False), bits(size, True))
    ]
    return steps + [[(d, d ^ 1) for d in range(size)]]


def turned(value, size, odd):
    count = size.bit_length() - 2
    back = value * 0
    for b in range(count):
        back = back | (((value >> b) & 1) << (count - 1 - b))
    return jnp.where(odd == 1, value, back)


def slot_of(index, place, size):
    mask = index ^ place
    low = mask & 1
    return low * (size // 2) + turned(mask >> 1, size, (place & 1) ^ low)


def index_of(slot, place, size):
    low = slot // (size // 2)
    return ((turned(slot % (size // 2), size, (place & 1) ^ low) << 1) | low) ^ place


def swap(value, step):
    return lax.ppermute(value, "dp", step)


def add_low(left, right):
    return (left.astype(WIDE) + right.astype(WIDE)).astype(LOW)


def across(piece, mask, size):
    return lax.ppermute(piece, "tensor", [(t, t ^ mask) for t in range(size)])


ORDER = (0, 2, 1, 3)


def to_others(piece, size):
    return [across(piece, m, size) for m in ORDER[1:]]


def nothing(*refs):
    pass


def after(value, *earlier):
    return pl.pallas_call(
        nothing,
        in_specs=[ANY] * (1 + len(earlier)),
        out_specs=ANY,
        out_shape=jax.ShapeDtypeStruct(value.shape, value.dtype),
        input_output_aliases={0: 0},
        cost_estimate=SMALL,
        name="after",
    )(value, *earlier)


def to_right(piece, size):
    return lax.ppermute(piece, "tensor", [(t, (t + 1) % size) for t in range(size)])


def to_left(piece, size):
    return lax.ppermute(piece, "tensor", [(t, (t - 1) % size) for t in range(size)])


def onward(pair, size):
    rows = pair[0].shape[0] // 2
    return to_right(pair[0][:rows], size), to_left(pair[1][rows:], size)


def assemble_near(me_ref, own_ref, left_ref, right_ref, out_ref):
    for step, piece_ref in enumerate((own_ref, left_ref, right_ref)):

        @pl.when(pl.program_id(0) == step)
        def _(piece_ref=piece_ref):
            out_ref[...] = piece_ref[...]


def assemble_far(me_ref, whole_ref, first_ref, second_ref, out_ref):
    rows = first_ref.shape[0]
    out_ref[:rows] = first_ref[...]
    out_ref[rows:] = second_ref[...]


def assembled(own, near, far):
    size = 4
    rows, width = own.shape
    full = pl.BlockSpec((rows, width), lambda g, me: (0, 0))
    part = pl.BlockSpec((rows // 2, width), lambda g, me: (0, 0))

    def turn(g):
        return jnp.where(g == 2, 1, -g)

    shape = jax.ShapeDtypeStruct((size * rows, width), own.dtype)
    me = lax.axis_index("tensor")[None]
    whole = pl.pallas_call(
        assemble_near,
        grid_spec=pltpu.PrefetchScalarGridSpec(
            num_scalar_prefetch=1,
            grid=(3,),
            in_specs=[full, full, full],
            out_specs=pl.BlockSpec(
                (rows, width), lambda g, me: (lax.rem(me[0] + turn(g) + size, size), 0)
            ),
        ),
        out_shape=shape,
        compiler_params=pltpu.CompilerParams(vmem_limit_bytes=VMEM),
        cost_estimate=SMALL,
        name="assemble_near",
    )(me, own, *near)
    return pl.pallas_call(
        assemble_far,
        grid_spec=pltpu.PrefetchScalarGridSpec(
            num_scalar_prefetch=1,
            grid=(1,),
            in_specs=[ANY, part, part],
            out_specs=pl.BlockSpec((rows, width), lambda g, me: (lax.rem(me[0] + 2, size), 0)),
        ),
        out_shape=shape,
        input_output_aliases={1: 0},
        compiler_params=pltpu.CompilerParams(vmem_limit_bytes=VMEM),
        cost_estimate=SMALL,
        name="assemble_far",
    )(me, whole, *far)


def pick(place_ref, in_ref, *refs):
    refs[-1][...] = in_ref[...].reshape(refs[-1].shape).astype(refs[-1].dtype)


def reorder_call(kernel, place, values, earlier, count, in_spec, out_spec, shape, dtype):
    return pl.pallas_call(
        kernel,
        grid_spec=pltpu.PrefetchScalarGridSpec(
            num_scalar_prefetch=1,
            grid=(count,),
            in_specs=[in_spec] * len(values) + [ANY] * len(earlier),
            out_specs=out_spec,
        ),
        out_shape=jax.ShapeDtypeStruct(shape, dtype),
        compiler_params=pltpu.CompilerParams(vmem_limit_bytes=VMEM),
        name="reorder",
    )(place[None], *values, *earlier)


def by_index(slots, place, dtype, *earlier):
    count, rows, width = slots.shape
    return reorder_call(
        pick,
        place,
        [slots],
        earlier,
        count,
        pl.BlockSpec((1, rows, width), lambda j, p: (slot_of(j, p[0], count), 0, 0)),
        pl.BlockSpec((1, rows, width), lambda j, p: (j, 0, 0)),
        slots.shape,
        dtype,
    )


def split_two(place_ref, in_ref, first_ref, second_ref):
    first_ref[0] = in_ref[0, 0].astype(first_ref.dtype)
    second_ref[0] = in_ref[1, 0].astype(second_ref.dtype)


def two_by_index(slots, place):
    _, count, rows, width = slots.shape
    one = pl.BlockSpec((1, rows, width), lambda j, p: (j, 0, 0))
    shape = (count, rows, width)
    return pl.pallas_call(
        split_two,
        grid_spec=pltpu.PrefetchScalarGridSpec(
            num_scalar_prefetch=1,
            grid=(count,),
            in_specs=[
                pl.BlockSpec((2, 1, rows, width), lambda j, p: (0, slot_of(j, p[0], count), 0, 0))
            ],
            out_specs=[one, one],
        ),
        out_shape=[jax.ShapeDtypeStruct(shape, LOW), jax.ShapeDtypeStruct(shape, WIDE)],
        compiler_params=pltpu.CompilerParams(vmem_limit_bytes=VMEM),
        name="reorder",
    )(place[None], slots)


def groups_by_index(slots, place):
    count, groups, rows, width = slots.shape
    return reorder_call(
        pick,
        place,
        [slots],
        (),
        count,
        pl.BlockSpec((1, groups, rows, width), lambda j, p: (slot_of(j, p[0], count), 0, 0, 0)),
        pl.BlockSpec((groups, 1, rows, width), lambda j, p: (0, j, 0, 0)),
        (groups, count, rows, width),
        LOW,
    )


def groups_by_slot(values, place, *earlier):
    groups, count, rows, width = values.shape
    return reorder_call(
        pick,
        place,
        [values],
        earlier,
        count,
        pl.BlockSpec((groups, 1, rows, width), lambda k, p: (0, index_of(k, p[0], count), 0, 0)),
        pl.BlockSpec((1, groups, rows, width), lambda k, p: (k, 0, 0, 0)),
        (count, groups, rows, width),
        LOW,
    )


def middle(
    attn_ref, w_out_ref, x_ref, dy_ref, rows_ref, w_ref, bias_ref,
    out_ref, mine_ref, theirs_ref, resid_ref, dw_out_ref, sums_ref, dw_ref, db_ref,
    a_ref, normed_ref, rstd_ref, mixed_ref, da_ref,
):
    @pl.when(pl.program_id(0) == 0)
    def _():
        resid = x_ref[...].astype(WIDE) + dot(attn_ref[...], w_out_ref[...], TN) + rows_ref[0:1]
        normed, rstd = norm_parts(resid)
        resid_ref[...] = resid
        normed_ref[...] = normed
        rstd_ref[...] = rstd
        a_ref[...] = (normed * rows_ref[1:2] + rows_ref[2:3]).astype(LOW)
        mixed_ref[...] = jnp.zeros_like(mixed_ref)
        da_ref[...] = jnp.zeros_like(da_ref)

    a_second, dy = a_ref[...], dy_ref[...]
    actives, d_uppers = [], []
    for lo in range(0, UNITS, BLOCK):
        some = slice(lo, lo + BLOCK)
        upper = dot(a_second, w_ref[0, some], NT) + bias_ref[:, some]
        square = upper * upper
        curve = jnp.tanh(0.7978845608028654 * (upper + 0.044715 * upper * square))
        rise = 0.5 * (1.0 + curve)
        active = (upper * rise).astype(LOW)
        slope = rise + 0.5 * upper * (1.0 - curve * curve) * (
            0.7978845608028654 * (1.0 + 3.0 * 0.044715 * square)
        )
        d_upper = dot(dy, w_ref[1, some], NT) * slope
        db_ref[:, some] = jnp.sum(d_upper, axis=0, keepdims=True)
        actives.append(active)
        d_uppers.append(d_upper.astype(LOW))
    active = jnp.concatenate(actives, axis=1)
    d_upper = jnp.concatenate(d_uppers, axis=1)
    mixed_ref[...] += dot(active, w_ref[1])
    da_ref[...] += dot(d_upper, w_ref[0])
    rows = dw_ref.shape[2]
    dw_ref[:, 0] = dot(d_upper, a_second, TN).astype(LOW).reshape(-1, rows, dw_ref.shape[3])
    dw_ref[:, 1] = dot(active, dy, TN).astype(LOW).reshape(-1, rows, dw_ref.shape[3])

    @pl.when(pl.program_id(0) == pl.num_programs(0) - 1)
    def _():
        out_ref[...] = (resid_ref[...] + mixed_ref[...] + rows_ref[3:4]).astype(LOW)
        d_resid, d_gain, d_bias = norm_back(
            normed_ref[...], rstd_ref[...], rows_ref[1:2], da_ref[...]
        )
        dy_wide = dy_ref[...].astype(WIDE)
        d_resid += dy_wide
        resid_ref[...] = d_resid
        sums_ref[0:1] = d_gain[None]
        sums_ref[1:2] = d_bias[None]
        sums_ref[2:3] = jnp.sum(d_resid, axis=0, keepdims=True)
        sums_ref[3:4] = jnp.sum(dy_wide, axis=0, keepdims=True)
        sums_ref[4:8] = jnp.zeros_like(sums_ref[4:8])
        low = d_resid.astype(LOW)
        split = mine_ref.shape[0]
        mine_ref[...] = dot(w_out_ref[:split], low, NT).astype(LOW)
        theirs_ref[...] = dot(w_out_ref[split:], low, NT).astype(LOW)
        dw_out_ref[...] = dot(attn_ref[...], low).astype(LOW)


def middle_call(attn, w_out, x, dy, rows, weights, bias, parts):
    tokens, width = x.shape
    hidden = weights.shape[1]
    once = pl.Buffered(1)

    def whole(*shape):
        return pl.BlockSpec(shape, lambda g: (0,) * len(shape), pipeline_mode=once)

    some = pl.BlockSpec((2, UNITS, width), lambda g: (0, g, 0))
    each = hidden // parts
    slots = pl.BlockSpec((UNITS // each, 2, each, width), lambda g: (g, 0, 0, 0))
    row = pl.BlockSpec((1, UNITS), lambda g: (0, g))
    local = attn.shape[0] // 2
    return pl.pallas_call(
        middle,
        grid=(hidden // UNITS,),
        in_specs=[
            whole(*attn.shape),
            whole(*w_out.shape),
            whole(tokens, width),
            whole(tokens, width),
            whole(*rows.shape),
            some,
            row,
        ],
        out_specs=[
            whole(tokens, width),
            whole(local, tokens),
            whole(local, tokens),
            whole(tokens, width),
            whole(*w_out.shape),
            whole(8, width),
            slots,
            row,
        ],
        out_shape=[
            jax.ShapeDtypeStruct((tokens, width), LOW),
            jax.ShapeDtypeStruct((local, tokens), LOW),
            jax.ShapeDtypeStruct((local, tokens), LOW),
            jax.ShapeDtypeStruct((tokens, width), WIDE),
            jax.ShapeDtypeStruct(w_out.shape, LOW),
            jax.ShapeDtypeStruct((8, width), WIDE),
            jax.ShapeDtypeStruct((parts, 2, each, width), LOW),
            jax.ShapeDtypeStruct((1, hidden), WIDE),
        ],
        scratch_shapes=[
            pltpu.VMEM((tokens, width), LOW),
            pltpu.VMEM((tokens, width), WIDE),
            pltpu.VMEM((tokens, 1), WIDE),
            pltpu.VMEM((tokens, width), WIDE),
            pltpu.VMEM((tokens, width), WIDE),
        ],
        compiler_params=pltpu.CompilerParams(vmem_limit_bytes=48 * 2**20),
        cost_estimate=SMALL,
        name="middle",
    )(attn, w_out, x, dy, rows, weights, bias)


def first_back(half_ref, d_a_ref, d_b_ref, w_a_ref, w_b_ref, *refs):
    mine_ref, theirs_ref = refs[-2:]
    own = mine_ref.shape[0]
    for out_ref, which in ((theirs_ref, 1 - half_ref[0]), (mine_ref, half_ref[0])):
        some = pl.ds(pl.multiple_of(which * own, own), own)
        value = dot(d_a_ref[:, some], w_a_ref[...], TN) + dot(d_b_ref[:, some], w_b_ref[...], TN)
        out_ref[...] = value.astype(out_ref.dtype)


def first_back_call(half, d_a, d_b, w_a, w_b, own, *earlier):
    width = w_a.shape[1]

    def whole(*shape):
        return pl.BlockSpec(shape, lambda g, h: (0,) * len(shape))

    return pl.pallas_call(
        first_back,
        grid_spec=pltpu.PrefetchScalarGridSpec(
            num_scalar_prefetch=1,
            grid=(1,),
            in_specs=[whole(*v.shape) for v in (d_a, d_b, w_a, w_b)] + [ANY] * len(earlier),
            out_specs=[whole(own, width), whole(own, width)],
        ),
        out_shape=[
            jax.ShapeDtypeStruct((own, width), WIDE),
            jax.ShapeDtypeStruct((own, width), LOW),
        ],
        compiler_params=pltpu.CompilerParams(vmem_limit_bytes=VMEM),
        cost_estimate=SMALL,
        name="first_back",
    )(half[None], d_a, d_b, w_a, w_b, *earlier)


def weight_back(place_ref, a_ref, d_a_ref, d_b_ref, *refs):
    refs[-1][0, 0] = dot(d_a_ref[0], a_ref[...]).astype(LOW)
    refs[-1][0, 1] = dot(d_b_ref[0], a_ref[...]).astype(LOW)


def weight_back_call(place, a_first, d_a, d_b, *earlier):
    count, rows, tokens = d_a.shape
    width = a_first.shape[1]
    piece = pl.BlockSpec((1, rows, tokens), lambda k, p: (index_of(k, p[0], count), 0, 0))
    return pl.pallas_call(
        weight_back,
        grid_spec=pltpu.PrefetchScalarGridSpec(
            num_scalar_prefetch=1,
            grid=(count,),
            in_specs=[pl.BlockSpec((tokens, width), lambda k, p: (0, 0)), piece, piece]
            + [ANY] * len(earlier),
            out_specs=pl.BlockSpec((1, 2, rows, width), lambda k, p: (k, 0, 0, 0)),
        ),
        out_shape=jax.ShapeDtypeStruct((count, 2, rows, width), LOW),
        compiler_params=pltpu.CompilerParams(vmem_limit_bytes=VMEM),
        cost_estimate=SMALL,
        name="weight_back",
    )(place[None], a_first, d_a, d_b, *earlier)


def shards(
    inputs,
    gain1,
    bias1,
    w_qkv,
    bias_q,
    bias_v,
    w_out,
    bias_out,
    gain2,
    bias2,
    w_fc,
    bias_fc,
    w_proj,
    bias_proj,
    cotangent,
):
    n_dp, n_t = lax.axis_size("dp"), lax.axis_size("tensor")
    place, me = lax.axis_index("dp"), lax.axis_index("tensor")
    count, width = inputs.shape
    local = w_qkv.shape[2]
    hidden = w_fc.shape[1]
    heads = local // HEAD
    scale = HEAD ** (-0.5)
    own = count // n_t
    half = lax.rem(me, 2)
    rows_q, rows_o, rows_f = 3 * local // n_dp, local // n_dp, hidden // n_dp

    plane = exchanges(n_dp)
    near, last = plane[:-1], plane[-1]

    qkv_own = w_qkv.transpose(1, 2, 0).reshape(3 * local, width)
    q = across(lax.dynamic_slice_in_dim(qkv_own, place * rows_q, rows_q, 0), 2, n_t)
    vector = across(jnp.concatenate([bias_q, bias_v, bias_fc]), 2, n_t)
    biases = [bias_fc, vector[2 * local :], across(bias_fc, 1, n_t), across(bias_fc, 3, n_t)]
    o = lax.dynamic_slice_in_dim(w_out, place * rows_o, rows_o, 0)
    o_parts = to_others(o, n_t)
    w = jnp.stack(
        [
            lax.dynamic_slice_in_dim(w_fc, place * rows_f, rows_f, 1).T,
            lax.dynamic_slice_in_dim(w_proj, place * rows_f, rows_f, 0),
        ]
    )
    w = lax.all_gather(w, ("dp", "tensor"), axis=1, tiled=True)

    x_seq = lax.dynamic_slice_in_dim(inputs, (me // 2) * LEN, LEN, 0).astype(WIDE)
    normed, _ = norm_parts(x_seq)
    a_first = (normed * gain1 + bias1).astype(LOW)

    def project(weight, add_q, add_v):
        proj = dot(weight, a_first, NT)
        query = (proj[:local] + add_q[:, None]) * scale
        values = proj[2 * local :] + add_v[:, None]
        proj = jnp.concatenate([query, proj[local : 2 * local], values], axis=0)
        return proj.astype(LOW).reshape(3, heads, HEAD, LEN)

    def halves(value):
        mine = lax.dynamic_slice_in_dim(value, half * own, own, value.ndim - 1)
        theirs = lax.dynamic_slice_in_dim(value, (1 - half) * own, own, value.ndim - 1)
        return mine, theirs

    def both(held, step, axis=0):
        return jnp.concatenate([held, swap(held, step)], axis=axis)

    q, o = q[None], jnp.stack([o] + o_parts)[None]
    for step in near:
        q = both(q, step)
    q_take = swap(q, last)
    proj_a = project(qkv_own, bias_q, bias_v)
    out_a, lse_a = attention(proj_a)
    mine_a, theirs_a = halves(out_a.reshape(local, LEN))
    theirs_a = across(theirs_a, 1, n_t)
    for step in plane:
        o = both(o, step)
    qkv_other = by_index(jnp.concatenate([q, q_take], axis=0), place, LOW)
    qkv_other = qkv_other.reshape(3 * local, width)
    proj_b = project(qkv_other, vector[:local], vector[local : 2 * local])
    out_b, lse_b = attention(proj_b)
    mine_b, theirs_b = halves(out_b.reshape(local, LEN))
    theirs_b = across(theirs_b, 1, n_t)
    w_out_all = groups_by_index(o, place).reshape(n_t * local, width)
    attn_low = jnp.concatenate([mine_a, mine_b, theirs_a, theirs_b], axis=0)
    place_of = jnp.array([ORDER.index(m) for m in range(n_t)], jnp.int32)
    place_of = place_of[jnp.arange(n_t, dtype=jnp.int32) ^ me]
    bias_fc_all = jnp.stack(biases).reshape(n_t, n_dp, rows_f)
    bias_fc_all = bias_fc_all.at[place_of].get(mode="promise_in_bounds")
    bias_fc_all = bias_fc_all.transpose(1, 0, 2).reshape(1, n_t * hidden)

    x_own = lax.dynamic_slice_in_dim(inputs, me * own, own, 0)
    dy = lax.dynamic_slice_in_dim(cotangent, me * own, own, 0)
    rows = jnp.stack([bias_out, gain2, bias2, bias_proj])
    output, d_mine, d_theirs, d_resid, o, sums_row, w, sums_fc = middle_call(
        attn_low, w_out_all, x_own, dy, rows, w, bias_fc_all, n_dp
    )
    from_left = to_right(output, n_t)
    d_take = across(d_theirs, 1, n_t)
    output_near = (from_left, to_left(after(output, d_take), n_t))

    def parted(held, axis=0):
        middle = held.shape[axis] // 2
        return jnp.split(held, [middle], axis=axis)

    def folded(held, taken, axis=0):
        held, taken = parted(held, axis), parted(taken, axis)
        return add_low(held[0], taken[0]), add_low(held[1], taken[1])

    w = lax.psum_scatter(w, "dp")
    d_out = jnp.where(
        half == 0,
        jnp.concatenate([d_mine, d_take], axis=1),
        jnp.concatenate([d_take, d_mine], axis=1),
    )
    d_out = d_out.reshape(2, heads, HEAD, LEN)

    down = near[::-1]
    d_proj_a = attention_back(proj_a, out_a, d_out[0], lse_a)
    d_proj_b = attention_back(proj_b, out_b, d_out[1], lse_b, d_proj_a)
    d_proj_a = d_proj_a.reshape(3 * local, LEN)
    d_proj_b = d_proj_b.reshape(3 * local, LEN)

    d_first, d_theirs = first_back_call(
        half, d_proj_a, d_proj_b, qkv_own, qkv_other, own, *output_near
    )
    d_first_take = across(d_theirs, 1, n_t)
    output_near = tuple(after(part, d_first_take) for part in output_near)
    output_far = onward(output_near, n_t)
    sums_a = jnp.sum(d_proj_a.reshape(3, local, LEN).astype(WIDE), axis=2)
    sums_b = jnp.sum(d_proj_b.reshape(3, local, LEN).astype(WIDE), axis=2)
    group = jnp.arange(n_t, dtype=jnp.int32)[None, :, None]
    bias_rows = jnp.where(group == me, sums_a[:, None], 0.0)
    bias_rows += jnp.where(group == (me ^ 2), sums_b[:, None], 0.0)
    sums_fc = after(sums_fc, d_first_take).reshape(n_dp, n_t, rows_f).transpose(1, 0, 2)
    w = w.reshape(2, n_t, rows_f, width)
    w = [lax.dynamic_index_in_dim(w, me ^ m, 1, keepdims=False) for m in ORDER]
    w_parts = [across(w[at], m, n_t) for at, m in enumerate(ORDER) if at]
    normed1, rstd1 = norm_parts(x_own.astype(WIDE))
    d_first = d_first + d_first_take.astype(WIDE)
    d_in_norm, d_gain1, d_bias1 = norm_back(normed1, rstd1, gain1, d_first)
    d_inputs = (d_resid + d_in_norm).astype(LOW)
    inputs_near = to_right(d_inputs, n_t), to_left(d_inputs, n_t)

    d_proj_a, d_proj_b = (d.reshape(n_dp, rows_q, LEN) for d in (d_proj_a, d_proj_b))
    q, q_send = parted(weight_back_call(place, a_first, d_proj_a, d_proj_b, d_inputs))
    q_take = swap(q_send, last)
    o, o_send = parted(groups_by_slot(o.reshape(n_t, n_dp, rows_o, width), place, d_inputs))
    o_take = swap(o_send, last)
    for step in down:
        q, q_send = folded(q, q_take)
        q_take = swap(q_send, step)
        o, o_send = folded(o, o_take)
        o_take = swap(o_send, step)

    def sum_tensor(held):
        return held[0], [across(held[at], m, n_t) for at, m in enumerate(ORDER) if at]

    def total_of(mine, parts):
        total = mine.astype(WIDE)
        for part in parts:
            total += part.astype(WIDE)
        return total.astype(LOW)

    w_parts[0] = after(w_parts[0], *output_far, *inputs_near)
    w = total_of(w[0], w_parts)[:, None]
    inputs_far = onward(inputs_near, n_t)
    o, o_parts = sum_tensor(add_low(o, after(o_take, w))[0])
    q = add_low(q, after(q_take, w))[0]
    q_take = across(q[1], 2, n_t)
    vectors = jnp.concatenate(
        [
            d_gain1,
            d_bias1,
            sums_row[:4].reshape(-1),
            bias_rows[0].reshape(-1),
            bias_rows[2].reshape(-1),
            sums_fc.reshape(-1),
        ]
    ).reshape(-1, 128)
    vectors = after(vectors, d_inputs)
    for step in plane:
        vectors = vectors + swap(vectors, step)
    vectors = after(vectors, w)
    vectors = vectors + across(vectors, 1, n_t)
    vectors = after(vectors, *inputs_far)
    vectors = vectors + across(vectors, 2, n_t)
    o = total_of(o, o_parts)[None]
    q = add_low(q[0], q_take)[None]
    for step in plane:
        o, q = both(o, step), both(q, step)
    for step in plane:
        w = both(w, step, 1)
    d_w_out = by_index(o, place, WIDE).reshape(local, width)
    d_w_qkv = by_index(q, place, WIDE).reshape(3, local, width).transpose(2, 0, 1)
    whole_output = assembled(output, output_near, output_far)
    whole_d_inputs = assembled(d_inputs, inputs_near, inputs_far)
    d_w_fc, d_w_proj = two_by_index(w, place)
    d_w_proj = d_w_proj.reshape(hidden, width)
    d_w_fc = d_w_fc.reshape(hidden, width).T.astype(WIDE)
    vectors = vectors.reshape(-1, width)
    d_gain1, d_bias1, d_gain2, d_bias2, d_bias_out, d_bias_proj = (vectors[r] for r in range(6))
    d_bias_q = lax.dynamic_slice_in_dim(vectors[6], me * local, local, 0)
    d_bias_v = lax.dynamic_slice_in_dim(vectors[7], me * local, local, 0)
    d_bias_fc = lax.dynamic_slice_in_dim(vectors[8:].reshape(-1), me * hidden, hidden, 0)
    return (
        whole_output,
        whole_d_inputs,
        d_gain1,
        d_bias1,
        d_w_qkv,
        d_bias_q,
        d_bias_v,
        d_w_out,
        d_bias_out,
        d_gain2,
        d_bias2,
        d_w_fc,
        d_bias_fc,
        d_w_proj,
        d_bias_proj,
    )


def solution(mesh):
    placed = (
        P("dp", None),
        P(),
        P(),
        P(None, None, "tensor"),
        P("tensor"),
        P("tensor"),
        P("tensor", None),
        P(),
        P(),
        P(),
        P(None, "tensor"),
        P("tensor"),
        P("tensor", None),
        P(),
        P("dp", None),
    )
    return jax.shard_map(
        shards,
        mesh=mesh,
        in_specs=placed,
        out_specs=(
            P("dp", None),
            P("dp", None),
            P(),
            P(),
            P(None, None, "tensor"),
            P("tensor"),
            P("tensor"),
            P("tensor", None),
            P(),
            P(),
            P(),
            P(None, "tensor"),
            P("tensor"),
            P("tensor", None),
            P(),
        ),
        check_vma=False,
    )
```

profile of v0, /device:TPU:0, one launch (start us, length us, event | category | flops | bytes accessed | tf_op | source)
XLA Modules:
  0.0 360.9 jit_solution(3119504279466010290)
XLA Ops:
  11.8 4.0 %collective-permute-start.7 = (bf16[24,768]{1,0:T(8,128)(2,1)}, bf16[24,768]{1,0:T(8,128)(2,1)}, u32[]{:S(2)}, u32[]{:S(2)}) collective-permute-start(bf16[24,768]{1,0:T(8,128)(2,1)} %constant_dynamic-slice_fusion.3), channel_id=1, source_target_pairs={{0,2},{1,3},{2,0},{3,1},{4,6},{5,7},{6,4},{7,5},{8,10},{9,11},{10,... | collective-permute-start | bytes 110600 | tf_op jit(solution)/shard_map/ppermute | solution.py:193
  15.9 1.6 collective-permute-start.8
  17.4 1.5 constant_dynamic-slice_fusion.7
  19.0 1.9 collective-permute-start
  20.9 2.5 collective-permute-start.13
  23.4 1.8 convert_reduce_fusion
  25.2 2.0 fusion.2
  30.0 5.0 %attention.2 = (bf16[3,64,1024]{2,1,0:T(8,128)(2,1)S(1)}, f32[3,1,1024]{2,1,0:T(1,128)S(1)}) custom-call(bf16[3,3,64,1024]{3,2,1,0:T(8,128)(2,1)S(1)} %bitcast.112, bf16[3,3,64,1024]{3,2,1,0:T(8,128)(2,1)S(1)} %bitcast.113, bf16[3,3,64,1024]{3,2,1,0:T(8,128)(2,1)S(1)} %bitcast.114), custom_call_target="tpu_custom_call" | custom-call | flops 1 | bytes 1 | tf_op jit(solution)/shard_map/attention/pallas_call | solution.py:122
  38.6 2.7 convert_reduce_fusion.3
  50.4 2.0 collective-permute-done.1
  53.3 1.6 collective-permute-start.2
  56.6 2.7 collective-permute-done.2
  60.4 2.8 collective-permute-start.5
  68.1 5.0 %attention.3 = (bf16[3,64,1024]{2,1,0:T(8,128)(2,1)S(1)}, f32[3,1,1024]{2,1,0:T(1,128)S(1)}) custom-call(bf16[3,3,64,1024]{3,2,1,0:T(8,128)(2,1)S(1)} %bitcast.118, bf16[3,3,64,1024]{3,2,1,0:T(8,128)(2,1)S(1)} %bitcast.119, bf16[3,3,64,1024]{3,2,1,0:T(8,128)(2,1)S(1)} %bitcast.120), custom_call_target="tpu_custom_call" | custom-call | flops 1 | bytes 1 | tf_op jit(solution)/shard_map/attention/pallas_call | solution.py:122
  78.1 12.8 %collective-permute-done.6 = bf16[192,512]{1,0:T(8,128)(2,1)} collective-permute-done((bf16[192,512]{1,0:T(8,128)(2,1)}, bf16[192,512]{1,0:T(8,128)(2,1)}, u32[]{:S(2)}, u32[]{:S(2)}) %collective-permute-start.6) | collective-permute-done | bytes 196640 | tf_op jit(solution)/shard_map/ppermute | solution.py:193
  90.8 2.0 pad_maximum_fusion.7.attn_ref
  92.8 8.0 %all-gather.2.cloned.1.call-done.w_ref = bf16[2,3072,768]{2,1,0:T(8,128)(2,1)} async-done(((bf16[2,96,768]{2,1,0:T(8,128)(2,1)}), bf16[2,3072,768]{2,1,0:T(8,128)(2,1)}) %all-gather.2.cloned.1.call-update) | async-done | bytes 9437200 | tf_op jit(solution)/shard_map/all_gather | solution.py:597
  103.7 26.0 %middle.1 = (bf16[512,768]{1,0:T(8,128)(2,1)}, bf16[384,512]{1,0:T(8,128)(2,1)S(1)}, bf16[384,512]{1,0:T(8,128)(2,1)S(1)}, f32[512,768]{1,0:T(8,128)}, bf16[768,...) custom-call(bf16[768,512]{1,0:T(8,128)(2,1)S(1)} %copy-done.24, ...), custom_call_target="tpu_custom_call" | custom-call | flops 1 | bytes 1 | tf_op jit(solution)/shard_map/middle/pallas_call | solution.py:451
  133.4 1.9 collective-permute-start.16
  135.8 2.1 copy.54.refs_0_
  138.0 7.0 %collective-permute-done.16.refs_1_ = bf16[384,512]{1,0:T(8,128)(2,1)S(1)} collective-permute-done((bf16[384,512]{1,0:T(8,128)(2,1)}, bf16[384,512]{1,0:T(8,128)(2,1)S(1)}, u32[]{:S(2)}, u32[]{:S(2)}) %collective-permute-start.16) | collective-permute-done | bytes 393248 | tf_op jit(solution)/shard_map/ppermute | solution.py:193
  145.8 1.7 collective-permute-start.17
  150.0 7.5 %attention_back.2.refs_0_ = bf16[3,3,64,1024]{3,2,1,0:T(8,128)(2,1)S(1)} custom-call(bf16[3,3,64,1024]{3,2,1,0:T(8,128)(2,1)S(1)} %bitcast.115, bf16[3,3,64,1024]{3,2,1,0:T(8,128)(2,1)S(1)} %bitcast.116, bf16[3,3,64,1024]{3,2,1,0:T(8,128)(2,1)S(1)} %bitcast.117, bf16[3,64,1024]{2,1,0:T(8,128)(2,1)S(1)} %get-tuple-element.31.o_ref, ...), custom_call_target="tpu_custom_call" | custom-call | flops 1 | bytes 1 | tf_op jit(solution)/shard_map/attention_back/pallas_call | solution.py:139
  157.6 7.3 %attention_back.3 = bf16[3,3,64,1024]{3,2,1,0:T(8,128)(2,1)S(1)} custom-call(bf16[3,3,64,1024]{3,2,1,0:T(8,128)(2,1)S(1)} %bitcast.121, bf16[3,3,64,1024]{3,2,1,0:T(8,128)(2,1)S(1)} %bitcast.122, bf16[3,3,64,1024]{3,2,1,0:T(8,128)(2,1)S(1)} %bitcast.123, bf16[3,64,1024]{2,1,0:T(8,128)(2,1)S(1)} %copy-done.30, bf16[3,64,1024]{2,1,0:T(8,128)(2,1)S(1)} %bitcast.133, ...), custom_call_target="tpu_custom_call" | custom-call | flops 1 | bytes 1 | tf_op jit(solution)/shard_map/attention_back/pallas_call | solution.py:139
  164.9 15.1 %collective-permute-done.17.refs_1_.refs_0_ = bf16[512,768]{1,0:T(8,128)(2,1)} collective-permute-done((bf16[512,768]{1,0:T(8,128)(2,1)}, bf16[512,768]{1,0:T(8,128)(2,1)}, u32[]{:S(2)}, u32[]{:S(2)}) %collective-permute-start.17) | collective-permute-done | bytes 786464 | tf_op jit(solution)/shard_map/ppermute | solution.py:224
  180.0 2.7 first_back.1
  186.4 17.0 %collective-permute-done.18.refs_1_ = bf16[512,768]{1,0:T(8,128)(2,1)} collective-permute-done((bf16[512,768]{1,0:T(8,128)(2,1)S(1)}, bf16[512,768]{1,0:T(8,128)(2,1)}, u32[]{:S(2)}, u32[]{:S(2)}) %collective-permute-start.18) | collective-permute-done | bytes 786464 | tf_op jit(solution)/shard_map/ppermute | solution.py:193
  203.4 2.6 fusion.16
  206.0 1.8 fusion.15.own_ref.refs_1_.refs_0_
  208.6 3.2 collective-permute-start.22
  215.5 5.4 %weight_back.1 = bf16[8,2,72,768]{3,2,1,0:T(8,128)(2,1)S(1)} custom-call(s32[1]{0:T(128)} %bitcast.6.place_ref, bf16[1024,768]{1,0:T(8,128)(2,1)S(1)} %copy-done.15, bf16[8,72,1024]{2,1,0:T(8,128)(2,1)S(1)} %bitcast.125, bf16[8,72,1024]{2,1,0:T(8,128)(2,1)S(1)} %bitcast.127, bf16[512,768]{1,0:T(8,128)(2,1)S(1)} %fusion.15.own_ref.refs_1_.refs_0_), custom_call_target="tpu_custom_call" | custom-call | flops 1 | bytes 1 | tf_op jit(solution)/shard_map/weight_back/pallas_call | solution.py:538
  227.3 2.7 collective-permute-done.25
  233.4 1.9 slice.170
  235.5 1.9 collective-permute-start.19
  237.4 2.3 add_convert_fusion.3
  241.4 2.3 add_convert_fusion.1
  243.7 1.8 collective-permute-done.22.right_ref.refs_4_
  246.9 1.8 slice.173
  248.6 4.2 %collective-permute-done.20.second_ref.refs_2_ = bf16[256,768]{1,0:T(8,128)(2,1)S(1)} collective-permute-done((bf16[256,768]{1,0:T(8,128)(2,1)S(1)}, bf16[256,768]{1,0:T(8,128)(2,1)S(1)}, u32[]{:S(2)}, u32[]{:S(2)}) %collective-permute-start.20) | collective-permute-done | bytes 393248 | tf_op jit(solution)/shard_map/ppermute | solution.py:224
  253.5 3.3 collective-permute-start.24
  256.9 3.5 assemble_near.2.whole_ref
  261.0 3.1 collective-permute-done.19.first_ref.refs_1_
  264.1 1.9 assemble_far.2
  266.0 3.0 assemble_near.3.whole_ref
  270.5 1.8 collective-permute-done.23.first_ref.refs_1_
  272.3 2.4 collective-permute-start.30
  274.8 1.6 add_convert_fusion.8
  276.4 3.0 collective-permute-done.24.second_ref.refs_2_
  279.4 1.7 collective-permute-start.42
  283.4 14.6 %collective-permute-done.28.refs_0_ = bf16[2,96,768]{2,1,0:T(8,128)(2,1)S(1)} collective-permute-done((bf16[2,96,768]{2,1,0:T(8,128)(2,1)S(1)}, bf16[2,96,768]{2,1,0:T(8,128)(2,1)S(1)}, u32[]{:S(2)}, u32[]{:S(2)}) %collective-permute-start.28) | collective-permute-done | bytes 294944 | tf_op jit(solution)/shard_map/ppermute | solution.py:193
  298.7 2.0 fusion.27.refs_1_
  303.9 5.3 %collective-permute-start.43 = (bf16[24,768]{1,0:T(8,128)(2,1)S(1)}, bf16[24,768]{1,0:T(8,128)(2,1)S(1)}, u32[]{:S(2)}, u32[]{:S(2)}) collective-permute-start(bf16[24,768]{1,0:T(8,128)(2,1)S(1)} %get-tuple-element.70), channel_id=1, source_target_pairs={{0,2},{1,3},{2,0},{3,1},{4,6},{5,7},{6,4},{7,5},{8,10},{9,11},{10,... | collective-permute-start | bytes 110600 | tf_op jit(solution)/shard_map/ppermute | solution.py:193
  309.6 2.3 collective-permute-start.45
  314.1 1.6 collective-permute-start.50
  319.2 1.9 collective-permute-start.32
  321.1 3.3 collective-permute-done.50
  328.1 2.9 collective-permute-done.37
  331.0 1.9 collective-permute-start.38
  334.8 2.2 collective-permute-done.38
  339.2 2.6 reorder.10
  341.9 2.9 reorder.8
  346.0 3.2 reorder.11
  349.3 1.6 bitcast_convert_fusion
  350.9 3.2 copy.49
  (356 shorter events, 88.7 us)
Async XLA Ops:
  7.2 34.1 %copy-start = (bf16[2048,768]{1,0:T(8,128)(2,1)S(1)}, bf16[2048,768]{1,0:T(8,128)(2,1)}, u32[]{:S(2)}) copy-start(bf16[2048,768]{1,0:T(8,128)(2,1)} %param.30) | copy-start | bytes 9437188
  7.2 13.7 %copy-start.69 = (f32[768]{0:T(1024)S(1)}, f32[768]{0:T(1024)}, u32[]{:S(2)}) copy-start(f32[768]{0:T(1024)} %param.27) | copy-start | bytes 9220
  7.2 93.5 %all-gather.2.cloned.1.call-start = ((), (), s32[]{:S(2)}) async-start(), calls=%async_computation.1 | async-start | bytes 9732096 | tf_op jit(solution)/shard_map/all_gather | solution.py:597
  10.4 258.7 %reduce-scatter.2.cloned.1.call-start = ((), (), s32[]{:S(2)}) async-start(), calls=%async_computation.2 | async-start | bytes 10616832 | tf_op jit(solution)/shard_map/reduce_scatter | solution.py:660
  11.8 34.0 %collective-permute-start.7 = (bf16[24,768]{1,0:T(8,128)(2,1)}, bf16[24,768]{1,0:T(8,128)(2,1)}, u32[]{:S(2)}, u32[]{:S(2)}) collective-permute-start(bf16[24,768]{1,0:T(8,128)(2,1)} %constant_dynamic-slice_fusion.3), channel_id=1, source_target_pairs={{0,2},{1,3},{2,0},{3,1},{4,6},{5,7},{6,4},{7,5},{8,10},{9,11},{10,... | collective-permute-start | bytes 110600 | tf_op jit(solution)/shard_map/ppermute | solution.py:193
  15.9 30.1 %collective-permute-start.8 = (bf16[24,768]{1,0:T(8,128)(2,1)}, bf16[24,768]{1,0:T(8,128)(2,1)}, u32[]{:S(2)}, u32[]{:S(2)}) collective-permute-start(bf16[24,768]{1,0:T(8,128)(2,1)} %constant_dynamic-slice_fusion.3), channel_id=1, source_target_pairs={{0,1},{1,0},{2,3},{3,2},{4,5},{5,4},{6,7},{7,6},{8,9},{9,8},{10,11... | collective-permute-start | bytes 110600 | tf_op jit(solution)/shard_map/ppermute | solution.py:193
  17.4 31.5 %collective-permute-start.9 = (bf16[24,768]{1,0:T(8,128)(2,1)}, bf16[24,768]{1,0:T(8,128)(2,1)}, u32[]{:S(2)}, u32[]{:S(2)}) collective-permute-start(bf16[24,768]{1,0:T(8,128)(2,1)} %constant_dynamic-slice_fusion.3), channel_id=1, source_target_pairs={{0,3},{1,2},{2,1},{3,0},{4,7},{5,6},{6,5},{7,4},{8,11},{9,10},{10,... | collective-permute-start | bytes 110600 | tf_op jit(solution)/shard_map/ppermute | solution.py:193
  19.0 28.4 %collective-permute-start = (bf16[72,768]{1,0:T(8,128)(2,1)}, bf16[72,768]{1,0:T(8,128)(2,1)}, u32[]{:S(2)}, u32[]{:S(2)}) collective-permute-start(bf16[72,768]{1,0:T(8,128)(2,1)} %constant_dynamic-slice_fusion.7), channel_id=1, source_target_pairs={{0,2},{1,3},{2,0},{3,1},{4,6},{5,7},{6,4},{7,5},{8,10},{9,11},{10,... | collective-permute-start | bytes 331784 | tf_op jit(solution)/shard_map/ppermute | solution.py:193
  20.9 39.5 %collective-permute-start.13 = (f32[768]{0:T(1024)S(1)}, f32[768]{0:T(1024)}, u32[]{:S(2)}, u32[]{:S(2)}) collective-permute-start(f32[768]{0:T(1024)S(1)} %copy-done.69), channel_id=1, source_target_pairs={{0,1},{1,0},{2,3},{3,2},{4,5},{5,4},{6,7},{7,6},{8,9},{9,8},{10,11... | collective-permute-start | bytes 9224 | tf_op jit(solution)/shard_map/ppermute | solution.py:193
  45.9 18.2 %collective-permute-start.14 = (f32[768]{0:T(1024)S(1)}, f32[768]{0:T(1024)S(1)}, u32[]{:S(2)}, u32[]{:S(2)}) collective-permute-start(f32[768]{0:T(1024)S(1)} %copy-done.69), channel_id=1, source_target_pairs={{0,3},{1,2},{2,1},{3,0},{4,7},{5,6},{6,5},{7,4},{8,11},{9,10},{10,... | collective-permute-start | bytes 9224 | tf_op jit(solution)/shard_map/ppermute | solution.py:193
  45.9 18.1 %collective-permute-start.4 = (f32[1152]{0:T(1024)S(1)}, f32[1152]{0:T(1024)S(1)}, u32[]{:S(2)}, u32[]{:S(2)}) collective-permute-start(f32[1152]{0:T(1024)S(1)} %concatenate.83), channel_id=1, source_target_pairs={{0,2},{1,3},{2,0},{3,1},{4,6},{5,7},{6,4},{7,5},{8,10},{9,11},{10,... | collective-permute-start | bytes 13832 | tf_op jit(solution)/shard_map/ppermute | solution.py:193
  47.4 5.0 %collective-permute-start.1 = (bf16[1,72,768]{2,1,0:T(8,128)(2,1)}, bf16[1,72,768]{2,1,0:T(8,128)(2,1)S(1)}, u32[]{:S(2)}, u32[]{:S(2)}) collective-permute-start(bf16[1,72,768]{2,1,0:T(8,128)(2,1)} %bitcast.8), channel_id=1, source_target_pairs={{0,16},{4,12},{8,24},{12,4},{16,0},{20,28},{24,8},{28,20},{1,17},{... | collective-permute-start | bytes 331784 | tf_op jit(solution)/shard_map/ppermute | solution.py:185
  49.8 14.5 %copy-start.48 = (bf16[1,4,24,768]{3,2,1,0:T(8,128)(2,1)}, bf16[1,4,24,768]{3,2,1,0:T(8,128)(2,1)S(1)}, u32[]{:S(2)}) copy-start(bf16[1,4,24,768]{3,2,1,0:T(8,128)(2,1)S(1)} %maximum_bitcast_fusion) | copy-start | bytes 442372
  49.8 5.7 %collective-permute-start.10 = (bf16[1,4,24,768]{3,2,1,0:T(8,128)(2,1)S(1)}, bf16[1,4,24,768]{3,2,1,0:T(8,128)(2,1)S(1)}, u32[]{:S(2)}, u32[]{:S(2)}) collective-permute-start(bf16[1,4,24,768]{3,2,1,0:T(8,128)(2,1)S(1)} %maximum_bitcast_fusion), channel_id=1, source_target_pairs={{0,16},{4,12},{8,24},{12,4},{16,0},{20,28},{24,8},{28,20},{1,17},{... | collective-permute-start | bytes 442376 | tf_op jit(solution)/shard_map/ppermute | solution.py:185
  53.3 6.0 %collective-permute-start.2 = (bf16[2,72,768]{2,1,0:T(8,128)(2,1)S(1)}, bf16[2,72,768]{2,1,0:T(8,128)(2,1)S(1)}, u32[]{:S(2)}, u32[]{:S(2)}) collective-permute-start(bf16[2,72,768]{2,1,0:T(8,128)(2,1)S(1)} %pad_maximum_fusion.15), channel_id=1, source_target_pairs={{0,8},{4,20},{8,0},{12,28},{16,24},{20,4},{24,16},{28,12},{1,9},{5... | collective-permute-start | bytes 663560 | tf_op jit(solution)/shard_map/ppermute | solution.py:185
  55.5 8.7 %collective-permute-start.11 = (bf16[2,4,24,768]{3,2,1,0:T(8,128)(2,1)S(1)}, bf16[2,4,24,768]{3,2,1,0:T(8,128)(2,1)S(1)}, u32[]{:S(2)}, u32[]{:S(2)}) collective-permute-start(bf16[2,4,24,768]{3,2,1,0:T(8,128)(2,1)S(1)} %pad_maximum_fusion.12), channel_id=1, source_target_pairs={{0,8},{4,20},{8,0},{12,28},{16,24},{20,4},{24,16},{28,12},{1,9},{5... | collective-permute-start | bytes 884744 | tf_op jit(solution)/shard_map/ppermute | solution.py:185
  60.2 4.7 %collective-permute-start.3 = (bf16[4,72,768]{2,1,0:T(8,128)(2,1)S(1)}, bf16[4,72,768]{2,1,0:T(8,128)(2,1)S(1)}, u32[]{:S(2)}, u32[]{:S(2)}) collective-permute-start(bf16[4,72,768]{2,1,0:T(8,128)(2,1)S(1)} %pad_maximum_fusion.10), channel_id=1, source_target_pairs={{0,4},{4,0},{8,12},{12,8},{16,20},{20,16},{24,28},{28,24},{1,5},{5... | collective-permute-start | bytes 1327112 | tf_op jit(solution)/shard_map/ppermute | solution.py:185
  60.4 17.6 %collective-permute-start.5 = (bf16[192,512]{1,0:T(8,128)(2,1)}, bf16[192,512]{1,0:T(8,128)(2,1)}, u32[]{:S(2)}, u32[]{:S(2)}) collective-permute-start(bf16[192,512]{1,0:T(8,128)(2,1)} %get-tuple-element.67), channel_id=1, source_target_pairs={{0,1},{1,0},{2,3},{3,2},{4,5},{5,4},{6,7},{7,6},{8,9},{9,8},{10,11... | collective-permute-start | bytes 589832 | tf_op jit(solution)/shard_map/ppermute | solution.py:193
  64.3 11.0 %collective-permute-start.12 = (bf16[4,4,24,768]{3,2,1,0:T(8,128)(2,1)S(1)}, bf16[4,4,24,768]{3,2,1,0:T(8,128)(2,1)}, u32[]{:S(2)}, u32[]{:S(2)}) collective-permute-start(bf16[4,4,24,768]{3,2,1,0:T(8,128)(2,1)S(1)} %pad_maximum_fusion.8), channel_id=1, source_target_pairs={{0,4},{4,0},{8,12},{12,8},{16,20},{20,16},{24,28},{28,24},{1,5},{5... | collective-permute-start | bytes 1769480 | tf_op jit(solution)/shard_map/ppermute | solution.py:185
  74.0 16.8 %collective-permute-start.6 = (bf16[192,512]{1,0:T(8,128)(2,1)}, bf16[192,512]{1,0:T(8,128)(2,1)}, u32[]{:S(2)}, u32[]{:S(2)}) collective-permute-start(bf16[192,512]{1,0:T(8,128)(2,1)} %get-tuple-element.69), channel_id=1, source_target_pairs={{0,1},{1,0},{2,3},{3,2},{4,5},{5,4},{6,7},{7,6},{8,9},{9,8},{10,11... | collective-permute-start | bytes 589832 | tf_op jit(solution)/shard_map/ppermute | solution.py:193
  76.6 14.2 %copy-start.61 = (bf16[192,512]{1,0:T(8,128)(2,1)S(1)}, bf16[192,512]{1,0:T(8,128)(2,1)}, u32[]{:S(2)}) copy-start(bf16[192,512]{1,0:T(8,128)(2,1)} %get-tuple-element.66) | copy-start | bytes 589828
  76.7 14.2 %copy-start.62 = (bf16[192,512]{1,0:T(8,128)(2,1)S(1)}, bf16[192,512]{1,0:T(8,128)(2,1)}, u32[]{:S(2)}) copy-start(bf16[192,512]{1,0:T(8,128)(2,1)} %get-tuple-element.68) | copy-start | bytes 589828
  76.7 24.1 %copy-start.4 = (bf16[512,768]{1,0:T(8,128)(2,1)S(1)}, bf16[512,768]{1,0:T(8,128)(2,1)}, u32[]{:S(2)}) copy-start(bf16[512,768]{1,0:T(8,128)(2,1)} %get-tuple-element.52.x_ref) | copy-start | bytes 2359300
  133.4 11.7 %collective-permute-start.16 = (bf16[384,512]{1,0:T(8,128)(2,1)}, bf16[384,512]{1,0:T(8,128)(2,1)S(1)}, u32[]{:S(2)}, u32[]{:S(2)}) collective-permute-start(bf16[384,512]{1,0:T(8,128)(2,1)} %copy-done.45), channel_id=1, source_target_pairs={{0,1},{1,0},{2,3},{3,2},{4,5},{5,4},{6,7},{7,6},{8,9},{9,8},{10,11... | collective-permute-start | bytes 1179656 | tf_op jit(solution)/shard_map/ppermute | solution.py:193
  135.8 12.2 %copy-start.70 = (f32[512]{0:T(512)S(1)}, f32[512]{0:T(512)}, u32[]{:S(2)}) copy-start(f32[512]{0:T(512)} %get-tuple-element.51) | copy-start | bytes 6148
  137.9 26.9 %collective-permute-start.15 = (bf16[512,768]{1,0:T(8,128)(2,1)}, bf16[512,768]{1,0:T(8,128)(2,1)}, u32[]{:S(2)}, u32[]{:S(2)}) collective-permute-start(bf16[512,768]{1,0:T(8,128)(2,1)} %get-tuple-element.33.own_ref), channel_id=1, source_target_pairs={{0,1},{1,2},{2,3},{3,0},{4,5},{5,6},{6,7},{7,4},{8,9},{9,10},{10,1... | collective-permute-start | bytes 2359304 | tf_op jit(solution)/shard_map/ppermute | solution.py:220
  145.8 34.1 %collective-permute-start.17 = (bf16[512,768]{1,0:T(8,128)(2,1)}, bf16[512,768]{1,0:T(8,128)(2,1)}, u32[]{:S(2)}, u32[]{:S(2)}) collective-permute-start(bf16[512,768]{1,0:T(8,128)(2,1)} %after.10), channel_id=1, source_target_pairs={{0,3},{1,0},{2,1},{3,2},{4,7},{5,4},{6,5},{7,6},{8,11},{9,8},{10,9... | collective-permute-start | bytes 2359304 | tf_op jit(solution)/shard_map/ppermute | solution.py:224
  157.5 22.4 %copy-start.22 = (bf16[8,72,768]{2,1,0:T(8,128)(2,1)S(1)}, bf16[8,72,768]{2,1,0:T(8,128)(2,1)}, u32[]{:S(2)}) copy-start(bf16[8,72,768]{2,1,0:T(8,128)(2,1)} %copy-done.21) | copy-start | bytes 2654212
  157.6 22.4 %copy-start.34 = (bf16[768,3,192]{0,2,1:T(8,128)(2,1)S(1)}, bf16[768,3,192]{0,2,1:T(8,128)(2,1)}, u32[]{:S(2)}) copy-start(bf16[768,3,192]{0,2,1:T(8,128)(2,1)} %param.19) | copy-start | bytes 2654212
  164.8 17.8 %copy-start.7 = (bf16[3,3,64,1024]{3,2,1,0:T(8,128)(2,1)}, bf16[3,3,64,1024]{3,2,1,0:T(8,128)(2,1)S(1)}, u32[]{:S(2)}) copy-start(bf16[3,3,64,1024]{3,2,1,0:T(8,128)(2,1)S(1)} %attention_back.3) | copy-start | bytes 3538948
  183.8 19.5 %collective-permute-start.18 = (bf16[512,768]{1,0:T(8,128)(2,1)S(1)}, bf16[512,768]{1,0:T(8,128)(2,1)}, u32[]{:S(2)}, u32[]{:S(2)}) collective-permute-start(bf16[512,768]{1,0:T(8,128)(2,1)S(1)} %get-tuple-element.38), channel_id=1, source_target_pairs={{0,1},{1,0},{2,3},{3,2},{4,5},{5,4},{6,7},{7,6},{8,9},{9,8},{10,11... | collective-permute-start | bytes 2359304 | tf_op jit(solution)/shard_map/ppermute | solution.py:193
  207.8 29.6 %collective-permute-start.21 = (bf16[512,768]{1,0:T(8,128)(2,1)S(1)}, bf16[512,768]{1,0:T(8,128)(2,1)S(1)}, u32[]{:S(2)}, u32[]{:S(2)}) collective-permute-start(bf16[512,768]{1,0:T(8,128)(2,1)S(1)} %fusion.15.own_ref.refs_1_.refs_0_), channel_id=1, source_target_pairs={{0,1},{1,2},{2,3},{3,0},{4,5},{5,6},{6,7},{7,4},{8,9},{9,10},{10,1... | collective-permute-start | bytes 2359304 | tf_op jit(solution)/shard_map/ppermute | solution.py:220
  208.6 36.8 %collective-permute-start.22 = (bf16[512,768]{1,0:T(8,128)(2,1)S(1)}, bf16[512,768]{1,0:T(8,128)(2,1)}, u32[]{:S(2)}, u32[]{:S(2)}) collective-permute-start(bf16[512,768]{1,0:T(8,128)(2,1)S(1)} %fusion.15.own_ref.refs_1_.refs_0_), channel_id=1, source_target_pairs={{0,3},{1,0},{2,1},{3,2},{4,7},{5,4},{6,5},{7,6},{8,11},{9,8},{10,9... | collective-permute-start | bytes 2359304 | tf_op jit(solution)/shard_map/ppermute | solution.py:224
  214.5 20.9 %collective-permute-start.40 = (bf16[4,4,24,768]{3,2,1,0:T(8,128)(2,1)}, bf16[4,4,24,768]{3,2,1,0:T(8,128)(2,1)}, u32[]{:S(2)}, u32[]{:S(2)}) collective-permute-start(bf16[4,4,24,768]{3,2,1,0:T(8,128)(2,1)} %split.84), channel_id=1, source_target_pairs={{0,4},{4,0},{8,12},{12,8},{16,20},{20,16},{24,28},{28,24},{1,5},{5... | collective-permute-start | bytes 1769480 | tf_op jit(solution)/shard_map/ppermute | solution.py:185
  223.1 18.3 %collective-permute-start.33 = (bf16[4,2,72,768]{3,2,1,0:T(8,128)(2,1)}, bf16[4,2,72,768]{3,2,1,0:T(8,128)(2,1)}, u32[]{:S(2)}, u32[]{:S(2)}) collective-permute-start(bf16[4,2,72,768]{3,2,1,0:T(8,128)(2,1)} %split.75), channel_id=1, source_target_pairs={{0,4},{4,0},{8,12},{12,8},{16,20},{20,16},{24,28},{28,24},{1,5},{5... | collective-permute-start | bytes 2654216 | tf_op jit(solution)/shard_map/ppermute | solution.py:185
  225.8 4.2 %collective-permute-start.25 = (f32[72,128]{1,0:T(8,128)}, f32[72,128]{1,0:T(8,128)S(1)}, u32[]{:S(2)}, u32[]{:S(2)}) collective-permute-start(f32[72,128]{1,0:T(8,128)} %after.14), channel_id=1, source_target_pairs={{0,16},{4,12},{8,24},{12,4},{16,0},{20,28},{24,8},{28,20},{1,17},{... | collective-permute-start | bytes 110600 | tf_op jit(solution)/shard_map/ppermute | solution.py:185
  230.8 4.5 %collective-permute-start.26 = (f32[72,128]{1,0:T(8,128)S(1)}, f32[72,128]{1,0:T(8,128)S(1)}, u32[]{:S(2)}, u32[]{:S(2)}) collective-permute-start(f32[72,128]{1,0:T(8,128)S(1)} %add.231), channel_id=1, source_target_pairs={{0,8},{4,20},{8,0},{12,28},{16,24},{20,4},{24,16},{28,12},{1,9},{5... | collective-permute-start | bytes 110600 | tf_op jit(solution)/shard_map/ppermute | solution.py:185
  235.3 17.5 %collective-permute-start.20 = (bf16[256,768]{1,0:T(8,128)(2,1)S(1)}, bf16[256,768]{1,0:T(8,128)(2,1)S(1)}, u32[]{:S(2)}, u32[]{:S(2)}) collective-permute-start(bf16[256,768]{1,0:T(8,128)(2,1)S(1)} %slice.171), channel_id=1, source_target_pairs={{0,3},{1,0},{2,1},{3,2},{4,7},{5,4},{6,5},{7,6},{8,11},{9,8},{10,9... | collective-permute-start | bytes 1179656 | tf_op jit(solution)/shard_map/ppermute | solution.py:224
  235.5 28.7 %collective-permute-start.19 = (bf16[256,768]{1,0:T(8,128)(2,1)}, bf16[256,768]{1,0:T(8,128)(2,1)}, u32[]{:S(2)}, u32[]{:S(2)}) collective-permute-start(bf16[256,768]{1,0:T(8,128)(2,1)} %slice.170), channel_id=1, source_target_pairs={{0,1},{1,2},{2,3},{3,0},{4,5},{5,6},{6,7},{7,4},{8,9},{9,10},{10,1... | collective-permute-start | bytes 1179656 | tf_op jit(solution)/shard_map/ppermute | solution.py:220
  237.4 3.1 collective-permute-start.27
  240.5 29.9 %collective-permute-start.41 = (bf16[2,4,24,768]{3,2,1,0:T(8,128)(2,1)}, bf16[2,4,24,768]{3,2,1,0:T(8,128)(2,1)}, u32[]{:S(2)}, u32[]{:S(2)}) collective-permute-start(bf16[2,4,24,768]{3,2,1,0:T(8,128)(2,1)} %get-tuple-element.60), channel_id=1, source_target_pairs={{0,8},{4,20},{8,0},{12,28},{16,24},{20,4},{24,16},{28,12},{1,9},{5... | collective-permute-start | bytes 884744 | tf_op jit(solution)/shard_map/ppermute | solution.py:185
  241.4 30.9 %collective-permute-start.23 = (bf16[256,768]{1,0:T(8,128)(2,1)}, bf16[256,768]{1,0:T(8,128)(2,1)S(1)}, u32[]{:S(2)}, u32[]{:S(2)}) collective-permute-start(bf16[256,768]{1,0:T(8,128)(2,1)} %slice.172), channel_id=1, source_target_pairs={{0,1},{1,2},{2,3},{3,0},{4,5},{5,6},{6,7},{7,4},{8,9},{9,10},{10,1... | collective-permute-start | bytes 1179656 | tf_op jit(solution)/shard_map/ppermute | solution.py:220
  245.4 36.6 %collective-permute-start.34 = (bf16[2,2,72,768]{3,2,1,0:T(8,128)(2,1)}, bf16[2,2,72,768]{3,2,1,0:T(8,128)(2,1)}, u32[]{:S(2)}, u32[]{:S(2)}) collective-permute-start(bf16[2,2,72,768]{3,2,1,0:T(8,128)(2,1)} %get-tuple-element.54), channel_id=1, source_target_pairs={{0,8},{4,20},{8,0},{12,28},{16,24},{20,4},{24,16},{28,12},{1,9},{5... | collective-permute-start | bytes 1327112 | tf_op jit(solution)/shard_map/ppermute | solution.py:185
  253.5 25.8 %collective-permute-start.24 = (bf16[256,768]{1,0:T(8,128)(2,1)}, bf16[256,768]{1,0:T(8,128)(2,1)S(1)}, u32[]{:S(2)}, u32[]{:S(2)}) collective-permute-start(bf16[256,768]{1,0:T(8,128)(2,1)} %slice.173), channel_id=1, source_target_pairs={{0,3},{1,0},{2,1},{3,2},{4,7},{5,4},{6,5},{7,6},{8,11},{9,8},{10,9... | collective-permute-start | bytes 1179656 | tf_op jit(solution)/shard_map/ppermute | solution.py:224
  270.3 27.7 %collective-permute-start.28 = (bf16[2,96,768]{2,1,0:T(8,128)(2,1)S(1)}, bf16[2,96,768]{2,1,0:T(8,128)(2,1)S(1)}, u32[]{:S(2)}, u32[]{:S(2)}) collective-permute-start(bf16[2,96,768]{2,1,0:T(8,128)(2,1)S(1)} %get-tuple-element.61), channel_id=1, source_target_pairs={{0,2},{1,3},{2,0},{3,1},{4,6},{5,7},{6,4},{7,5},{8,10},{9,11},{10,... | collective-permute-start | bytes 884744 | tf_op jit(solution)/shard_map/ppermute | solution.py:193
  270.4 28.3 %collective-permute-start.29 = (bf16[2,96,768]{2,1,0:T(8,128)(2,1)S(1)}, bf16[2,96,768]{2,1,0:T(8,128)(2,1)S(1)}, u32[]{:S(2)}, u32[]{:S(2)}) collective-permute-start(bf16[2,96,768]{2,1,0:T(8,128)(2,1)S(1)} %get-tuple-element.63), channel_id=1, source_target_pairs={{0,1},{1,0},{2,3},{3,2},{4,5},{5,4},{6,7},{7,6},{8,9},{9,8},{10,11... | collective-permute-start | bytes 884744 | tf_op jit(solution)/shard_map/ppermute | solution.py:193
  272.3 26.4 %collective-permute-start.30 = (bf16[2,96,768]{2,1,0:T(8,128)(2,1)S(1)}, bf16[2,96,768]{2,1,0:T(8,128)(2,1)}, u32[]{:S(2)}, u32[]{:S(2)}) collective-permute-start(bf16[2,96,768]{2,1,0:T(8,128)(2,1)S(1)} %get-tuple-element.62), channel_id=1, source_target_pairs={{0,3},{1,2},{2,1},{3,0},{4,7},{5,6},{6,5},{7,4},{8,11},{9,10},{10,... | collective-permute-start | bytes 884744 | tf_op jit(solution)/shard_map/ppermute | solution.py:193
  279.4 22.8 %collective-permute-start.42 = (bf16[1,4,24,768]{3,2,1,0:T(8,128)(2,1)}, bf16[1,4,24,768]{3,2,1,0:T(8,128)(2,1)S(1)}, u32[]{:S(2)}, u32[]{:S(2)}) collective-permute-start(bf16[1,4,24,768]{3,2,1,0:T(8,128)(2,1)} %add_convert_fusion.8), channel_id=1, source_target_pairs={{0,16},{4,12},{8,24},{12,4},{16,0},{20,28},{24,8},{28,20},{1,17},{... | collective-permute-start | bytes 442376 | tf_op jit(solution)/shard_map/ppermute | solution.py:185
  283.1 28.8 %collective-permute-start.35 = (bf16[1,2,72,768]{3,2,1,0:T(8,128)(2,1)S(1)}, bf16[1,2,72,768]{3,2,1,0:T(8,128)(2,1)S(1)}, u32[]{:S(2)}, u32[]{:S(2)}) collective-permute-start(bf16[1,2,72,768]{3,2,1,0:T(8,128)(2,1)S(1)} %add_convert_fusion.5), channel_id=1, source_target_pairs={{0,16},{4,12},{8,24},{12,4},{16,0},{20,28},{24,8},{28,20},{1,17},{... | collective-permute-start | bytes 663560 | tf_op jit(solution)/shard_map/ppermute | solution.py:185
  300.8 12.3 %collective-permute-start.49 = (bf16[2,1,96,768]{3,2,1,0:T(8,128)(2,1)}, bf16[2,1,96,768]{3,2,1,0:T(8,128)(2,1)S(1)}, u32[]{:S(2)}, u32[]{:S(2)}) collective-permute-start(bf16[2,1,96,768]{3,2,1,0:T(8,128)(2,1)} %fusion.27.refs_1_), channel_id=1, source_target_pairs={{0,16},{4,12},{8,24},{12,4},{16,0},{20,28},{24,8},{28,20},{1,17},{... | collective-permute-start | bytes 884744 | tf_op jit(solution)/shard_map/ppermute | solution.py:185
  303.9 14.7 %collective-permute-start.43 = (bf16[24,768]{1,0:T(8,128)(2,1)S(1)}, bf16[24,768]{1,0:T(8,128)(2,1)S(1)}, u32[]{:S(2)}, u32[]{:S(2)}) collective-permute-start(bf16[24,768]{1,0:T(8,128)(2,1)S(1)} %get-tuple-element.70), channel_id=1, source_target_pairs={{0,2},{1,3},{2,0},{3,1},{4,6},{5,7},{6,4},{7,5},{8,10},{9,11},{10,... | collective-permute-start | bytes 110600 | tf_op jit(solution)/shard_map/ppermute | solution.py:193
  309.3 9.3 %collective-permute-start.44 = (bf16[24,768]{1,0:T(8,128)(2,1)S(1)}, bf16[24,768]{1,0:T(8,128)(2,1)S(1)}, u32[]{:S(2)}, u32[]{:S(2)}) collective-permute-start(bf16[24,768]{1,0:T(8,128)(2,1)S(1)} %get-tuple-element.72), channel_id=1, source_target_pairs={{0,1},{1,0},{2,3},{3,2},{4,5},{5,4},{6,7},{7,6},{8,9},{9,8},{10,11... | collective-permute-start | bytes 110600 | tf_op jit(solution)/shard_map/ppermute | solution.py:193
  309.6 9.0 %collective-permute-start.45 = (bf16[24,768]{1,0:T(8,128)(2,1)S(1)}, bf16[24,768]{1,0:T(8,128)(2,1)S(1)}, u32[]{:S(2)}, u32[]{:S(2)}) collective-permute-start(bf16[24,768]{1,0:T(8,128)(2,1)S(1)} %get-tuple-element.71), channel_id=1, source_target_pairs={{0,3},{1,2},{2,1},{3,0},{4,7},{5,6},{6,5},{7,4},{8,11},{9,10},{10,... | collective-permute-start | bytes 110600 | tf_op jit(solution)/shard_map/ppermute | solution.py:193
  311.9 5.0 %collective-permute-start.31 = (f32[72,128]{1,0:T(8,128)}, f32[72,128]{1,0:T(8,128)S(1)}, u32[]{:S(2)}, u32[]{:S(2)}) collective-permute-start(f32[72,128]{1,0:T(8,128)} %after.16), channel_id=1, source_target_pairs={{0,1},{1,0},{2,3},{3,2},{4,5},{5,4},{6,7},{7,6},{8,9},{9,8},{10,11... | collective-permute-start | bytes 110600 | tf_op jit(solution)/shard_map/ppermute | solution.py:193
  314.1 10.3 %collective-permute-start.50 = (bf16[2,2,96,768]{3,2,1,0:T(8,128)(2,1)S(1)}, bf16[2,2,96,768]{3,2,1,0:T(8,128)(2,1)S(1)}, u32[]{:S(2)}, u32[]{:S(2)}) collective-permute-start(bf16[2,2,96,768]{3,2,1,0:T(8,128)(2,1)S(1)} %pad_maximum_fusion.9), channel_id=1, source_target_pairs={{0,8},{4,20},{8,0},{12,28},{16,24},{20,4},{24,16},{28,12},{1,9},{5... | collective-permute-start | bytes 1769480 | tf_op jit(solution)/shard_map/ppermute | solution.py:185
  316.9 8.9 %collective-permute-start.36 = (bf16[72,768]{1,0:T(8,128)(2,1)S(1)}, bf16[72,768]{1,0:T(8,128)(2,1)S(1)}, u32[]{:S(2)}, u32[]{:S(2)}) collective-permute-start(bf16[72,768]{1,0:T(8,128)(2,1)S(1)} %slice_bitcast_fusion), channel_id=1, source_target_pairs={{0,2},{1,3},{2,0},{3,1},{4,6},{5,7},{6,4},{7,5},{8,10},{9,11},{10,... | collective-permute-start | bytes 331784 | tf_op jit(solution)/shard_map/ppermute | solution.py:193
  318.6 7.9 %collective-permute-start.46 = (bf16[1,24,768]{2,1,0:T(8,128)(2,1)S(1)}, bf16[1,24,768]{2,1,0:T(8,128)(2,1)S(1)}, u32[]{:S(2)}, u32[]{:S(2)}) collective-permute-start(bf16[1,24,768]{2,1,0:T(8,128)(2,1)S(1)} %fusion.33), channel_id=1, source_target_pairs={{0,16},{4,12},{8,24},{12,4},{16,0},{20,28},{24,8},{28,20},{1,17},{... | collective-permute-start | bytes 110600 | tf_op jit(solution)/shard_map/ppermute | solution.py:185
  319.2 8.9 %collective-permute-start.32 = (f32[72,128]{1,0:T(8,128)}, f32[72,128]{1,0:T(8,128)S(1)}, u32[]{:S(2)}, u32[]{:S(2)}) collective-permute-start(f32[72,128]{1,0:T(8,128)} %after.17), channel_id=1, source_target_pairs={{0,2},{1,3},{2,0},{3,1},{4,6},{5,7},{6,4},{7,5},{8,10},{9,11},{10,... | collective-permute-start | bytes 110600 | tf_op jit(solution)/shard_map/ppermute | solution.py:193
  325.7 19.1 %collective-permute-start.51 = (bf16[2,4,96,768]{3,2,1,0:T(8,128)(2,1)S(1)}, bf16[2,4,96,768]{3,2,1,0:T(8,128)(2,1)S(1)}, u32[]{:S(2)}, u32[]{:S(2)}) collective-permute-start(bf16[2,4,96,768]{3,2,1,0:T(8,128)(2,1)S(1)} %pad_maximum_fusion.4), channel_id=1, source_target_pairs={{0,4},{4,0},{8,12},{12,8},{16,20},{20,16},{24,28},{28,24},{1,5},{5... | collective-permute-start | bytes 3538952 | tf_op jit(solution)/shard_map/ppermute | solution.py:185
  325.9 5.1 %collective-permute-start.37 = (bf16[1,72,768]{2,1,0:T(8,128)(2,1)S(1)}, bf16[1,72,768]{2,1,0:T(8,128)(2,1)S(1)}, u32[]{:S(2)}, u32[]{:S(2)}) collective-permute-start(bf16[1,72,768]{2,1,0:T(8,128)(2,1)S(1)} %fusion.29), channel_id=1, source_target_pairs={{0,16},{4,12},{8,24},{12,4},{16,0},{20,28},{24,8},{28,20},{1,17},{... | collective-permute-start | bytes 331784 | tf_op jit(solution)/shard_map/ppermute | solution.py:185
  326.6 10.6 %collective-permute-start.47 = (bf16[2,24,768]{2,1,0:T(8,128)(2,1)S(1)}, bf16[2,24,768]{2,1,0:T(8,128)(2,1)S(1)}, u32[]{:S(2)}, u32[]{:S(2)}) collective-permute-start(bf16[2,24,768]{2,1,0:T(8,128)(2,1)S(1)} %pad_maximum_fusion.18), channel_id=1, source_target_pairs={{0,8},{4,20},{8,0},{12,28},{16,24},{20,4},{24,16},{28,12},{1,9},{5... | collective-permute-start | bytes 221192 | tf_op jit(solution)/shard_map/ppermute | solution.py:185
  331.0 6.0 %collective-permute-start.38 = (bf16[2,72,768]{2,1,0:T(8,128)(2,1)S(1)}, bf16[2,72,768]{2,1,0:T(8,128)(2,1)S(1)}, u32[]{:S(2)}, u32[]{:S(2)}) collective-permute-start(bf16[2,72,768]{2,1,0:T(8,128)(2,1)S(1)} %pad_maximum_fusion.16), channel_id=1, source_target_pairs={{0,8},{4,20},{8,0},{12,28},{16,24},{20,4},{24,16},{28,12},{1,9},{5... | collective-permute-start | bytes 663560 | tf_op jit(solution)/shard_map/ppermute | solution.py:185
  337.1 4.7 %collective-permute-start.39 = (bf16[4,72,768]{2,1,0:T(8,128)(2,1)S(1)}, bf16[4,72,768]{2,1,0:T(8,128)(2,1)S(1)}, u32[]{:S(2)}, u32[]{:S(2)}) collective-permute-start(bf16[4,72,768]{2,1,0:T(8,128)(2,1)S(1)} %pad_maximum_fusion.11), channel_id=1, source_target_pairs={{0,4},{4,0},{8,12},{12,8},{16,20},{20,16},{24,28},{28,24},{1,5},{5... | collective-permute-start | bytes 1327112 | tf_op jit(solution)/shard_map/ppermute | solution.py:185
  337.2 2.0 collective-permute-start.48
  (69 other events, 234.3 us)
Sparse Core Ops, SparseCore 0:
  11.1 89.5 all-gather.1
  132.6 76.0 reduce-scatter.1
where the time goes:
time: 363 us; the launch traced here: 361 us
  waiting for transfers between devices  105 us (29%)
  Pallas kernels  78.1 us (22%)
  starting transfers between devices  64.3 us (18%)
  local copies, waits for them, and re-layouts  50.5 us (14%)
  other arithmetic  45.6 us (13%)
  between operations  15.1 us (4%)
    ppermute x20, waiting for transfers between devices, across(): return lax.ppermute(piece, 'tensor', [(t, t ^ mask) for t in range(size)])  51.4 us
    ppermute x20, starting transfers between devices, across(): return lax.ppermute(piece, 'tensor', [(t, t ^ mask) for t in range(size)])  32.2 us
    pallas_call x1, Pallas kernels, middle_call(): pl.pallas_call(middle, grid=(hidden // UNITS,), in_specs=[whole(*attn.sha...  26 us
    ppermute x4, waiting for transfers between devices, to_left(): lax.ppermute(piece, 'tensor', [(t, (t - 1) % size) for t in range(size)])  24.1 us
    ppermute x24, starting transfers between devices, swap(): return lax.ppermute(value, 'dp', step)  20.8 us
    unnamed x165, local copies, waits for them, and re-layouts  20.8 us
    ppermute x24, waiting for transfers between devices, swap(): return lax.ppermute(value, 'dp', step)  16.7 us
    pallas_call x2, Pallas kernels, attention_back(): pl.pallas_call(attend_back, grid=(heads,), in_specs=QKV + [PER_HEAD, PER_...  14.7 us
  transfers between devices with their start and end apart: 54, of which 18 were waited for; matrix products, arithmetic and copies ran while one was open for 20% of the time, Pallas kernels for 14%

commit v1 on v0

--- a/solution.py
+++ b/solution.py
@@ -342,6 +342,46 @@
         compiler_params=pltpu.CompilerParams(vmem_limit_bytes=VMEM),
         name="reorder",
     )(place[None], slots)
+
+
+def turn_two(place_ref, *refs):
+    first_ref, second_ref = refs[-2:]
+    pieces = [ref[:, 0].astype(WIDE) for ref in refs[:-2]]
+    first_ref[...] = jnp.concatenate([piece[0] for piece in pieces], axis=0).T
+    second_ref[...] = jnp.concatenate([piece[1] for piece in pieces], axis=0)
+
+
+def turned_by_index(slots, place):
+    _, count, rows, width = slots.shape
+    if 4 * rows % 128:
+        first, second = two_by_index(slots, place)
+        first = first.reshape(count * rows, width).T.astype(WIDE)
+        return first, second.reshape(count * rows, width)
+
+    def piece(at):
+        return pl.BlockSpec(
+            (2, 1, rows, width), lambda g, p: (0, slot_of(4 * g + at, p[0], count), 0, 0)
+        )
+
+    return pl.pallas_call(
+        turn_two,
+        grid_spec=pltpu.PrefetchScalarGridSpec(
+            num_scalar_prefetch=1,
+            grid=(count // 4,),
+            in_specs=[piece(at) for at in range(4)],
+            out_specs=[
+                pl.BlockSpec((width, 4 * rows), lambda g, p: (0, g)),
+                pl.BlockSpec((4 * rows, width), lambda g, p: (g, 0)),
+            ],
+        ),
+        out_shape=[
+            jax.ShapeDtypeStruct((width, count * rows), WIDE),
+            jax.ShapeDtypeStruct((count * rows, width), WIDE),
+        ],
+        compiler_params=pltpu.CompilerParams(vmem_limit_bytes=VMEM),
+        cost_estimate=SMALL,
+        name="reorder",
+    )(place[None], slots, slots, slots, slots)
 
 
 def groups_by_index(slots, place):
@@ -487,7 +527,7 @@
             pltpu.VMEM((tokens, width), WIDE),
             pltpu.VMEM((tokens, width), WIDE),
         ],
-        compiler_params=pltpu.CompilerParams(vmem_limit_bytes=48 * 2**20),
+        compiler_params=pltpu.CompilerParams(vmem_limit_bytes=56 * 2**20),
         cost_estimate=SMALL,
         name="middle",
     )(attn, w_out, x, dy, rows, weights, bias)
@@ -672,7 +712,7 @@
     d_proj_b = d_proj_b.reshape(3 * local, LEN)
 
     d_first, d_theirs = first_back_call(
-        half, d_proj_a, d_proj_b, qkv_own, qkv_other, own, *output_near
+        half, d_proj_a, d_proj_b, qkv_own, qkv_other, own
     )
     d_first_take = across(d_theirs, 1, n_t)
     output_near = tuple(after(part, d_first_take) for part in output_near)
@@ -688,7 +728,7 @@
     w_parts = [across(w[at], m, n_t) for at, m in enumerate(ORDER) if at]
     normed1, rstd1 = norm_parts(x_own.astype(WIDE))
     d_first = d_first + d_first_take.astype(WIDE)
-    d_in_norm, d_gain1, d_bias1 = norm_back(normed1, rstd1, gain1, d_first)
+    d_in_norm, d_gain1, d_bias1 = norm_back(normed1, rstd1, after(gain1, *output_near), d_first)
     d_inputs = (d_resid + d_in_norm).astype(LOW)
     inputs_near = to_right(d_inputs, n_t), to_left(d_inputs, n_t)
 
@@ -745,9 +785,7 @@
     d_w_qkv = by_index(q, place, WIDE).reshape(3, local, width).transpose(2, 0, 1)
     whole_output = assembled(output, output_near, output_far)
     whole_d_inputs = assembled(d_inputs, inputs_near, inputs_far)
-    d_w_fc, d_w_proj = two_by_index(w, place)
-    d_w_proj = d_w_proj.reshape(hidden, width)
-    d_w_fc = d_w_fc.reshape(hidden, width).T.astype(WIDE)
+    d_w_fc, d_w_proj = turned_by_index(w, place)
     vectors = vectors.reshape(-1, width)
     d_gain1, d_bias1, d_gain2, d_bias2, d_bias_out, d_bias_proj = (vectors[r] for r in range(6))
     d_bias_q = lax.dynamic_slice_in_dim(vectors[6], me * local, local, 0)

time: 363 us -> 352 us (0.970)
  waiting for transfers between devices: 105 us -> 89 us
  starting transfers between devices: 64.3 us -> 77.5 us
  local copies, waits for them, and re-layouts: 50.5 us -> 45.2 us
    ppermute x4, waiting for transfers between devices: 24.1 us -> 13.5 us  [to_left(): lax.ppermute(piece, 'tensor', [(t, (t - 1) % size) for t in range(size)])]
    ppermute x4, starting transfers between devices: 8.37 us -> 15.6 us  [to_left(): lax.ppermute(piece, 'tensor', [(t, (t - 1) % size) for t in range(size)])]
    ppermute x4, waiting for transfers between devices: 4.94 us -> 0.01 us  [to_right(): lax.ppermute(piece, 'tensor', [(t, (t + 1) % size) for t in range(size)])]
    unnamed x165 -> x126, local copies, waits for them, and re-layouts: 20.8 us -> 16.1 us
  transfers between devices with their start and end apart: 54 -> 54, of which waited for: 18 -> 17; matrix products, arithmetic and copies ran while one was open for 20% -> 21% of each run, Pallas kernels for 14% -> 13%
where the time goes in v1:
time: 352 us; the launch traced here: 350 us
  waiting for transfers between devices  89 us (25%)
  Pallas kernels  78.3 us (22%)
  starting transfers between devices  77.5 us (22%)
  local copies, waits for them, and re-layouts  45.2 us (13%)
  other arithmetic  43.1 us (12%)
  between operations  15 us (4%)
    ppermute x20, waiting for transfers between devices, across(): return lax.ppermute(piece, 'tensor', [(t, t ^ mask) for t in range(size)])  52.8 us
    ppermute x20, starting transfers between devices, across(): return lax.ppermute(piece, 'tensor', [(t, t ^ mask) for t in range(size)])  35.4 us
    pallas_call x1, Pallas kernels, middle_call(): pl.pallas_call(middle, grid=(hidden // UNITS,), in_specs=[whole(*attn.sha...  27.4 us
    ppermute x24, starting transfers between devices, swap(): return lax.ppermute(value, 'dp', step)  22.8 us
    ppermute x24, waiting for transfers between devices, swap(): return lax.ppermute(value, 'dp', step)  16.9 us
    unnamed x126, local copies, waits for them, and re-layouts  16.1 us
    ppermute x4, starting transfers between devices, to_left(): lax.ppermute(piece, 'tensor', [(t, (t - 1) % size) for t in range(size)])  15.6 us
    pallas_call x2, Pallas kernels, attention_back(): pl.pallas_call(attend_back, grid=(heads,), in_specs=QKV + [PER_HEAD, PER_...  14.7 us
  transfers between devices with their start and end apart: 54, of which 17 were waited for; matrix products, arithmetic and copies ran while one was open for 21% of the time, Pallas kernels for 13%

profile of v1, /device:TPU:0, one launch (start us, length us, event | category | flops | bytes accessed | tf_op | source)
XLA Modules:
  0.0 350.4 jit_solution(8256259429854877118)
XLA Ops:
  12.6 4.0 %collective-permute-start.7 = (bf16[24,768]{1,0:T(8,128)(2,1)}, bf16[24,768]{1,0:T(8,128)(2,1)}, u32[]{:S(2)}, u32[]{:S(2)}) collective-permute-start(bf16[24,768]{1,0:T(8,128)(2,1)} %constant_dynamic-slice_fusion.3), channel_id=1, source_target_pairs={{0,2},{1,3},{2,0},{3,1},{4,6},{5,7},{6,4},{7,5},{8,10},{9,11},{10,... | collective-permute-start | bytes 110600 | tf_op jit(solution)/shard_map/ppermute | solution.py:193
  16.6 1.6 collective-permute-start.8
  18.2 1.5 constant_dynamic-slice_fusion.7
  19.7 1.9 collective-permute-start
  21.6 2.5 collective-permute-start.13
  24.1 1.8 convert_reduce_fusion
  25.9 2.0 fusion.2
  30.7 5.0 %attention.2 = (bf16[3,64,1024]{2,1,0:T(8,128)(2,1)S(1)}, f32[3,1,1024]{2,1,0:T(1,128)S(1)}) custom-call(bf16[3,3,64,1024]{3,2,1,0:T(8,128)(2,1)S(1)} %bitcast.107, bf16[3,3,64,1024]{3,2,1,0:T(8,128)(2,1)S(1)} %bitcast.108, bf16[3,3,64,1024]{3,2,1,0:T(8,128)(2,1)S(1)} %bitcast.109), custom_call_target="tpu_custom_call" | custom-call | flops 1 | bytes 1 | tf_op jit(solution)/shard_map/attention/pallas_call | solution.py:122
  39.4 2.7 convert_reduce_fusion.3
  48.9 1.5 collective-permute-start.1
  51.8 2.0 collective-permute-done.1
  54.8 1.6 collective-permute-start.2
  58.4 2.3 collective-permute-done.2
  62.6 2.9 collective-permute-start.5
  70.3 5.0 %attention.3 = (bf16[3,64,1024]{2,1,0:T(8,128)(2,1)S(1)}, f32[3,1,1024]{2,1,0:T(1,128)S(1)}) custom-call(bf16[3,3,64,1024]{3,2,1,0:T(8,128)(2,1)S(1)} %bitcast.113, bf16[3,3,64,1024]{3,2,1,0:T(8,128)(2,1)S(1)} %bitcast.114, bf16[3,3,64,1024]{3,2,1,0:T(8,128)(2,1)S(1)} %bitcast.115), custom_call_target="tpu_custom_call" | custom-call | flops 1 | bytes 1 | tf_op jit(solution)/shard_map/attention/pallas_call | solution.py:122
  80.7 2.1 collective-permute-done.5
  82.8 12.5 %collective-permute-done.6 = bf16[192,512]{1,0:T(8,128)(2,1)S(1)} collective-permute-done((bf16[192,512]{1,0:T(8,128)(2,1)S(1)}, bf16[192,512]{1,0:T(8,128)(2,1)S(1)}, u32[]{:S(2)}, u32[]{:S(2)}) %collective-permute-start.6) | collective-permute-done | bytes 196640 | tf_op jit(solution)/shard_map/ppermute | solution.py:193
  95.2 1.9 pad_maximum_fusion.7.attn_ref
  97.1 5.8 %all-gather.2.cloned.1.call-done.w_ref = bf16[2,3072,768]{2,1,0:T(8,128)(2,1)} async-done(((bf16[2,96,768]{2,1,0:T(8,128)(2,1)}), bf16[2,3072,768]{2,1,0:T(8,128)(2,1)}) %all-gather.2.cloned.1.call-update) | async-done | bytes 9437200 | tf_op jit(solution)/shard_map/all_gather | solution.py:637
  102.9 27.4 %middle.1 = (bf16[512,768]{1,0:T(8,128)(2,1)}, bf16[384,512]{1,0:T(8,128)(2,1)}, bf16[384,512]{1,0:T(8,128)(2,1)}, f32[512,768]{1,0:T(8,128)}, bf16[768,768]{1,0...) custom-call(bf16[768,512]{1,0:T(8,128)(2,1)} %pad_maximum_fusion.7.attn_ref, ...), custom_call_target="tpu_custom_call" | custom-call | flops 1 | bytes 1 | tf_op jit(solution)/shard_map/middle/pallas_call | solution.py:491
  132.8 2.1 copy.54.refs_0_
  136.0 7.0 %collective-permute-done.16.refs_1_ = bf16[384,512]{1,0:T(8,128)(2,1)S(1)} collective-permute-done((bf16[384,512]{1,0:T(8,128)(2,1)S(1)}, bf16[384,512]{1,0:T(8,128)(2,1)S(1)}, u32[]{:S(2)}, u32[]{:S(2)}) %collective-permute-start.16) | collective-permute-done | bytes 393248 | tf_op jit(solution)/shard_map/ppermute | solution.py:193
  143.8 1.5 collective-permute-start.18
  146.9 7.5 %attention_back.2.refs_0_ = bf16[3,3,64,1024]{3,2,1,0:T(8,128)(2,1)S(1)} custom-call(bf16[3,3,64,1024]{3,2,1,0:T(8,128)(2,1)S(1)} %bitcast.110, bf16[3,3,64,1024]{3,2,1,0:T(8,128)(2,1)S(1)} %bitcast.111, bf16[3,3,64,1024]{3,2,1,0:T(8,128)(2,1)S(1)} %bitcast.112, bf16[3,64,1024]{2,1,0:T(8,128)(2,1)S(1)} %get-tuple-element.31.o_ref, ...), custom_call_target="tpu_custom_call" | custom-call | flops 1 | bytes 1 | tf_op jit(solution)/shard_map/attention_back/pallas_call | solution.py:139
  154.4 7.3 %attention_back.3 = bf16[3,3,64,1024]{3,2,1,0:T(8,128)(2,1)S(1)} custom-call(bf16[3,3,64,1024]{3,2,1,0:T(8,128)(2,1)S(1)} %bitcast.116, bf16[3,3,64,1024]{3,2,1,0:T(8,128)(2,1)S(1)} %bitcast.117, bf16[3,3,64,1024]{3,2,1,0:T(8,128)(2,1)S(1)} %bitcast.118, bf16[3,64,1024]{2,1,0:T(8,128)(2,1)S(1)} %copy-done.23, bf16[3,64,1024]{2,1,0:T(8,128)(2,1)S(1)} %bitcast.128, ...), custom_call_target="tpu_custom_call" | custom-call | flops 1 | bytes 1 | tf_op jit(solution)/shard_map/attention_back/pallas_call | solution.py:139
  161.7 2.7 first_back.1
  166.1 1.5 fusion.17
  168.3 8.6 %collective-permute-done.18.refs_0_ = bf16[512,768]{1,0:T(8,128)(2,1)} collective-permute-done((bf16[512,768]{1,0:T(8,128)(2,1)}, bf16[512,768]{1,0:T(8,128)(2,1)}, u32[]{:S(2)}, u32[]{:S(2)}) %collective-permute-start.18) | collective-permute-done | bytes 786464 | tf_op jit(solution)/shard_map/ppermute | solution.py:224
  176.9 16.7 %collective-permute-done.17.refs_1_ = bf16[512,768]{1,0:T(8,128)(2,1)} collective-permute-done((bf16[512,768]{1,0:T(8,128)(2,1)S(1)}, bf16[512,768]{1,0:T(8,128)(2,1)}, u32[]{:S(2)}, u32[]{:S(2)}) %collective-permute-start.17) | collective-permute-done | bytes 786464 | tf_op jit(solution)/shard_map/ppermute | solution.py:193
  194.8 3.2 fusion.16
  198.0 2.3 fusion.15.own_ref.refs_1_.refs_0_
  201.7 3.2 collective-permute-start.22
  208.0 5.4 %weight_back.1 = bf16[8,2,72,768]{3,2,1,0:T(8,128)(2,1)S(1)} custom-call(s32[1]{0:T(128)} %bitcast.6.place_ref, bf16[1024,768]{1,0:T(8,128)(2,1)S(1)} %copy-done.12, bf16[8,72,1024]{2,1,0:T(8,128)(2,1)S(1)} %bitcast.120, bf16[8,72,1024]{2,1,0:T(8,128)(2,1)S(1)} %bitcast.122, bf16[512,768]{1,0:T(8,128)(2,1)S(1)} %fusion.15.own_ref.refs_1_.refs_0_), custom_call_target="tpu_custom_call" | custom-call | flops 1 | bytes 1 | tf_op jit(solution)/shard_map/weight_back/pallas_call | solution.py:578
  218.7 2.0 collective-permute-start.25
  220.6 2.2 collective-permute-done.25
  223.6 1.9 collective-permute-start.26
  226.6 1.9 slice.170
  228.8 1.8 collective-permute-start.19
  230.6 1.9 add_convert_fusion.3
  232.5 1.8 slice.172
  235.4 2.1 add_convert_fusion.1
  238.8 1.9 collective-permute-start.34
  240.7 1.8 slice.173
  242.5 3.5 collective-permute-done.20.second_ref.refs_2_
  245.9 10.5 %collective-permute-start.24 = (bf16[256,768]{1,0:T(8,128)(2,1)}, bf16[256,768]{1,0:T(8,128)(2,1)S(1)}, u32[]{:S(2)}, u32[]{:S(2)}) collective-permute-start(bf16[256,768]{1,0:T(8,128)(2,1)} %slice.173), channel_id=1, source_target_pairs={{0,3},{1,0},{2,1},{3,2},{4,7},{5,4},{6,5},{7,6},{8,11},{9,8},{10,9... | collective-permute-start | bytes 1179656 | tf_op jit(solution)/shard_map/ppermute | solution.py:224
  256.5 3.5 assemble_near.2.whole_ref
  262.1 3.2 assemble_near.3.whole_ref
  267.5 1.7 collective-permute-start.29
  269.2 2.9 collective-permute-start.30
  276.3 9.6 %collective-permute-done.28.refs_0_ = bf16[2,96,768]{2,1,0:T(8,128)(2,1)S(1)} collective-permute-done((bf16[2,96,768]{2,1,0:T(8,128)(2,1)S(1)}, bf16[2,96,768]{2,1,0:T(8,128)(2,1)S(1)}, u32[]{:S(2)}, u32[]{:S(2)}) %collective-permute-start.28) | collective-permute-done | bytes 294944 | tf_op jit(solution)/shard_map/ppermute | solution.py:193
  286.7 4.9 %collective-permute-done.30 = bf16[2,96,768]{2,1,0:T(8,128)(2,1)} collective-permute-done((bf16[2,96,768]{2,1,0:T(8,128)(2,1)S(1)}, bf16[2,96,768]{2,1,0:T(8,128)(2,1)}, u32[]{:S(2)}, u32[]{:S(2)}) %collective-permute-start.30) | collective-permute-done | bytes 294944 | tf_op jit(solution)/shard_map/ppermute | solution.py:193
  291.6 2.1 fusion.27.refs_1_
  293.7 1.9 collective-permute-start.49
  297.3 5.6 %collective-permute-start.43 = (bf16[24,768]{1,0:T(8,128)(2,1)S(1)}, bf16[24,768]{1,0:T(8,128)(2,1)S(1)}, u32[]{:S(2)}, u32[]{:S(2)}) collective-permute-start(bf16[24,768]{1,0:T(8,128)(2,1)S(1)} %get-tuple-element.70), channel_id=1, source_target_pairs={{0,2},{1,3},{2,0},{3,1},{4,6},{5,7},{6,4},{7,5},{8,10},{9,11},{10,... | collective-permute-start | bytes 110600 | tf_op jit(solution)/shard_map/ppermute | solution.py:193
  304.2 2.3 collective-permute-start.45
  313.5 1.9 collective-permute-start.32
  315.5 3.6 %collective-permute-done.50 = bf16[2,2,96,768]{3,2,1,0:T(8,128)(2,1)S(1)} collective-permute-done((bf16[2,2,96,768]{3,2,1,0:T(8,128)(2,1)S(1)}, bf16[2,2,96,768]{3,2,1,0:T(8,128)(2,1)S(1)}, u32[]{:S(2)}, u32[]{:S(2)}) %collective-permute-start.50) | collective-permute-done | bytes 589856 | tf_op jit(solution)/shard_map/ppermute | solution.py:185
  320.4 1.9 collective-permute-start.47
  322.3 3.4 collective-permute-done.37
  325.7 1.5 collective-permute-start.38
  329.1 2.6 collective-permute-done.38
  333.9 2.6 reorder.10
  337.8 2.9 reorder.8
  340.7 2.7 reorder.11
  (316 shorter events, 84.0 us)
Async XLA Ops:
  7.2 34.9 %copy-start = (bf16[2048,768]{1,0:T(8,128)(2,1)S(1)}, bf16[2048,768]{1,0:T(8,128)(2,1)}, u32[]{:S(2)}) copy-start(bf16[2048,768]{1,0:T(8,128)(2,1)} %param.30) | copy-start | bytes 9437188
  7.2 95.7 %all-gather.2.cloned.1.call-start = ((), (), s32[]{:S(2)}) async-start(), calls=%async_computation.1 | async-start | bytes 9732096 | tf_op jit(solution)/shard_map/all_gather | solution.py:637
  8.1 19.9 %copy-start.43 = (f32[768]{0:T(1024)}, f32[768]{0:T(1024)S(1)}, u32[]{:S(2)}) copy-start(f32[768]{0:T(1024)S(1)} %copy.73.refs_0_) | copy-start | bytes 9220
  11.1 254.3 %reduce-scatter.2.cloned.1.call-start = ((), (), s32[]{:S(2)}) async-start(), calls=%async_computation.2 | async-start | bytes 10616832 | tf_op jit(solution)/shard_map/reduce_scatter | solution.py:700
  12.6 34.8 %collective-permute-start.7 = (bf16[24,768]{1,0:T(8,128)(2,1)}, bf16[24,768]{1,0:T(8,128)(2,1)}, u32[]{:S(2)}, u32[]{:S(2)}) collective-permute-start(bf16[24,768]{1,0:T(8,128)(2,1)} %constant_dynamic-slice_fusion.3), channel_id=1, source_target_pairs={{0,2},{1,3},{2,0},{3,1},{4,6},{5,7},{6,4},{7,5},{8,10},{9,11},{10,... | collective-permute-start | bytes 110600 | tf_op jit(solution)/shard_map/ppermute | solution.py:193
  16.6 30.9 %collective-permute-start.8 = (bf16[24,768]{1,0:T(8,128)(2,1)}, bf16[24,768]{1,0:T(8,128)(2,1)}, u32[]{:S(2)}, u32[]{:S(2)}) collective-permute-start(bf16[24,768]{1,0:T(8,128)(2,1)} %constant_dynamic-slice_fusion.3), channel_id=1, source_target_pairs={{0,1},{1,0},{2,3},{3,2},{4,5},{5,4},{6,7},{7,6},{8,9},{9,8},{10,11... | collective-permute-start | bytes 110600 | tf_op jit(solution)/shard_map/ppermute | solution.py:193
  18.2 32.2 %collective-permute-start.9 = (bf16[24,768]{1,0:T(8,128)(2,1)}, bf16[24,768]{1,0:T(8,128)(2,1)}, u32[]{:S(2)}, u32[]{:S(2)}) collective-permute-start(bf16[24,768]{1,0:T(8,128)(2,1)} %constant_dynamic-slice_fusion.3), channel_id=1, source_target_pairs={{0,3},{1,2},{2,1},{3,0},{4,7},{5,6},{6,5},{7,4},{8,11},{9,10},{10,... | collective-permute-start | bytes 110600 | tf_op jit(solution)/shard_map/ppermute | solution.py:193
  19.7 29.2 %collective-permute-start = (bf16[72,768]{1,0:T(8,128)(2,1)}, bf16[72,768]{1,0:T(8,128)(2,1)}, u32[]{:S(2)}, u32[]{:S(2)}) collective-permute-start(bf16[72,768]{1,0:T(8,128)(2,1)} %constant_dynamic-slice_fusion.7), channel_id=1, source_target_pairs={{0,2},{1,3},{2,0},{3,1},{4,6},{5,7},{6,4},{7,5},{8,10},{9,11},{10,... | collective-permute-start | bytes 331784 | tf_op jit(solution)/shard_map/ppermute | solution.py:193
  21.6 40.9 %collective-permute-start.13 = (f32[768]{0:T(1024)}, f32[768]{0:T(1024)}, u32[]{:S(2)}, u32[]{:S(2)}) collective-permute-start(f32[768]{0:T(1024)} %param.27), channel_id=1, source_target_pairs={{0,1},{1,0},{2,3},{3,2},{4,5},{5,4},{6,7},{7,6},{8,9},{9,8},{10,11... | collective-permute-start | bytes 9224 | tf_op jit(solution)/shard_map/ppermute | solution.py:193
  47.4 18.8 %collective-permute-start.14 = (f32[768]{0:T(1024)}, f32[768]{0:T(1024)S(1)}, u32[]{:S(2)}, u32[]{:S(2)}) collective-permute-start(f32[768]{0:T(1024)} %param.27), channel_id=1, source_target_pairs={{0,3},{1,2},{2,1},{3,0},{4,7},{5,6},{6,5},{7,4},{8,11},{9,10},{10,... | collective-permute-start | bytes 9224 | tf_op jit(solution)/shard_map/ppermute | solution.py:193
  47.4 18.8 %collective-permute-start.4 = (f32[1152]{0:T(1024)S(1)}, f32[1152]{0:T(1024)S(1)}, u32[]{:S(2)}, u32[]{:S(2)}) collective-permute-start(f32[1152]{0:T(1024)S(1)} %concatenate.83), channel_id=1, source_target_pairs={{0,2},{1,3},{2,0},{3,1},{4,6},{5,7},{6,4},{7,5},{8,10},{9,11},{10,... | collective-permute-start | bytes 13832 | tf_op jit(solution)/shard_map/ppermute | solution.py:193
  48.9 5.0 %collective-permute-start.1 = (bf16[1,72,768]{2,1,0:T(8,128)(2,1)}, bf16[1,72,768]{2,1,0:T(8,128)(2,1)S(1)}, u32[]{:S(2)}, u32[]{:S(2)}) collective-permute-start(bf16[1,72,768]{2,1,0:T(8,128)(2,1)} %bitcast.8), channel_id=1, source_target_pairs={{0,16},{4,12},{8,24},{12,4},{16,0},{20,28},{24,8},{28,20},{1,17},{... | collective-permute-start | bytes 331784 | tf_op jit(solution)/shard_map/ppermute | solution.py:185
  51.2 5.7 %collective-permute-start.10 = (bf16[1,4,24,768]{3,2,1,0:T(8,128)(2,1)S(1)}, bf16[1,4,24,768]{3,2,1,0:T(8,128)(2,1)S(1)}, u32[]{:S(2)}, u32[]{:S(2)}) collective-permute-start(bf16[1,4,24,768]{3,2,1,0:T(8,128)(2,1)S(1)} %maximum_bitcast_fusion), channel_id=1, source_target_pairs={{0,16},{4,12},{8,24},{12,4},{16,0},{20,28},{24,8},{28,20},{1,17},{... | collective-permute-start | bytes 442376 | tf_op jit(solution)/shard_map/ppermute | solution.py:185
  54.8 6.0 %collective-permute-start.2 = (bf16[2,72,768]{2,1,0:T(8,128)(2,1)S(1)}, bf16[2,72,768]{2,1,0:T(8,128)(2,1)S(1)}, u32[]{:S(2)}, u32[]{:S(2)}) collective-permute-start(bf16[2,72,768]{2,1,0:T(8,128)(2,1)S(1)} %pad_maximum_fusion.15), channel_id=1, source_target_pairs={{0,8},{4,20},{8,0},{12,28},{16,24},{20,4},{24,16},{28,12},{1,9},{5... | collective-permute-start | bytes 663560 | tf_op jit(solution)/shard_map/ppermute | solution.py:185
  57.0 9.4 %collective-permute-start.11 = (bf16[2,4,24,768]{3,2,1,0:T(8,128)(2,1)S(1)}, bf16[2,4,24,768]{3,2,1,0:T(8,128)(2,1)S(1)}, u32[]{:S(2)}, u32[]{:S(2)}) collective-permute-start(bf16[2,4,24,768]{3,2,1,0:T(8,128)(2,1)S(1)} %pad_maximum_fusion.12), channel_id=1, source_target_pairs={{0,8},{4,20},{8,0},{12,28},{16,24},{20,4},{24,16},{28,12},{1,9},{5... | collective-permute-start | bytes 884744 | tf_op jit(solution)/shard_map/ppermute | solution.py:185
  61.7 5.8 %collective-permute-start.3 = (bf16[4,72,768]{2,1,0:T(8,128)(2,1)S(1)}, bf16[4,72,768]{2,1,0:T(8,128)(2,1)S(1)}, u32[]{:S(2)}, u32[]{:S(2)}) collective-permute-start(bf16[4,72,768]{2,1,0:T(8,128)(2,1)S(1)} %pad_maximum_fusion.10), channel_id=1, source_target_pairs={{0,4},{4,0},{8,12},{12,8},{16,20},{20,16},{24,28},{28,24},{1,5},{5... | collective-permute-start | bytes 1327112 | tf_op jit(solution)/shard_map/ppermute | solution.py:185
  62.6 20.2 %collective-permute-start.5 = (bf16[192,512]{1,0:T(8,128)(2,1)}, bf16[192,512]{1,0:T(8,128)(2,1)}, u32[]{:S(2)}, u32[]{:S(2)}) collective-permute-start(bf16[192,512]{1,0:T(8,128)(2,1)} %get-tuple-element.67), channel_id=1, source_target_pairs={{0,1},{1,0},{2,3},{3,2},{4,5},{5,4},{6,7},{7,6},{8,9},{9,8},{10,11... | collective-permute-start | bytes 589832 | tf_op jit(solution)/shard_map/ppermute | solution.py:193
  67.3 10.8 %collective-permute-start.12 = (bf16[4,4,24,768]{3,2,1,0:T(8,128)(2,1)}, bf16[4,4,24,768]{3,2,1,0:T(8,128)(2,1)}, u32[]{:S(2)}, u32[]{:S(2)}) collective-permute-start(bf16[4,4,24,768]{3,2,1,0:T(8,128)(2,1)} %pad_maximum_fusion.8), channel_id=1, source_target_pairs={{0,4},{4,0},{8,12},{12,8},{16,20},{20,16},{24,28},{28,24},{1,5},{5... | collective-permute-start | bytes 1769480 | tf_op jit(solution)/shard_map/ppermute | solution.py:185
  76.2 19.1 %collective-permute-start.6 = (bf16[192,512]{1,0:T(8,128)(2,1)S(1)}, bf16[192,512]{1,0:T(8,128)(2,1)S(1)}, u32[]{:S(2)}, u32[]{:S(2)}) collective-permute-start(bf16[192,512]{1,0:T(8,128)(2,1)S(1)} %get-tuple-element.69), channel_id=1, source_target_pairs={{0,1},{1,0},{2,3},{3,2},{4,5},{5,4},{6,7},{7,6},{8,9},{9,8},{10,11... | collective-permute-start | bytes 589832 | tf_op jit(solution)/shard_map/ppermute | solution.py:193
  79.3 15.9 %copy-start.36 = (bf16[192,512]{1,0:T(8,128)(2,1)S(1)}, bf16[192,512]{1,0:T(8,128)(2,1)}, u32[]{:S(2)}) copy-start(bf16[192,512]{1,0:T(8,128)(2,1)} %get-tuple-element.66) | copy-start | bytes 589828
  131.4 11.7 %collective-permute-start.16 = (bf16[384,512]{1,0:T(8,128)(2,1)S(1)}, bf16[384,512]{1,0:T(8,128)(2,1)S(1)}, u32[]{:S(2)}, u32[]{:S(2)}) collective-permute-start(bf16[384,512]{1,0:T(8,128)(2,1)S(1)} %copy-done.58), channel_id=1, source_target_pairs={{0,1},{1,0},{2,3},{3,2},{4,5},{5,4},{6,7},{7,6},{8,9},{9,8},{10,11... | collective-permute-start | bytes 1179656 | tf_op jit(solution)/shard_map/ppermute | solution.py:193
  132.8 12.5 %copy-start.38 = (bf16[384,512]{1,0:T(8,128)(2,1)S(1)}, bf16[384,512]{1,0:T(8,128)(2,1)}, u32[]{:S(2)}) copy-start(bf16[384,512]{1,0:T(8,128)(2,1)} %get-tuple-element.34) | copy-start | bytes 1179652
  134.9 58.7 %collective-permute-start.15 = (bf16[512,768]{1,0:T(8,128)(2,1)}, bf16[512,768]{1,0:T(8,128)(2,1)}, u32[]{:S(2)}, u32[]{:S(2)}) collective-permute-start(bf16[512,768]{1,0:T(8,128)(2,1)} %get-tuple-element.33.own_ref), channel_id=1, source_target_pairs={{0,1},{1,2},{2,3},{3,0},{4,5},{5,6},{6,7},{7,4},{8,9},{9,10},{10,1... | collective-permute-start | bytes 2359304 | tf_op jit(solution)/shard_map/ppermute | solution.py:220
  143.8 33.1 %collective-permute-start.18 = (bf16[512,768]{1,0:T(8,128)(2,1)}, bf16[512,768]{1,0:T(8,128)(2,1)}, u32[]{:S(2)}, u32[]{:S(2)}) collective-permute-start(bf16[512,768]{1,0:T(8,128)(2,1)} %after.12), channel_id=1, source_target_pairs={{0,3},{1,0},{2,1},{3,2},{4,7},{5,4},{6,5},{7,6},{8,11},{9,8},{10,9... | collective-permute-start | bytes 2359304 | tf_op jit(solution)/shard_map/ppermute | solution.py:224
  146.9 7.5 %copy-start.28 = (f32[3,1,1024]{2,1,0:T(1,128)S(1)}, f32[3,1,1024]{2,1,0:T(1,128)}, u32[]{:S(2)}) copy-start(f32[3,1,1024]{2,1,0:T(1,128)} %copy-done.27) | copy-start | bytes 36868
  165.5 28.1 %collective-permute-start.17 = (bf16[512,768]{1,0:T(8,128)(2,1)S(1)}, bf16[512,768]{1,0:T(8,128)(2,1)}, u32[]{:S(2)}, u32[]{:S(2)}) collective-permute-start(bf16[512,768]{1,0:T(8,128)(2,1)S(1)} %get-tuple-element.38), channel_id=1, source_target_pairs={{0,1},{1,0},{2,3},{3,2},{4,5},{5,4},{6,7},{7,6},{8,9},{9,8},{10,11... | collective-permute-start | bytes 2359304 | tf_op jit(solution)/shard_map/ppermute | solution.py:193
  200.3 7.7 %copy-start.4 = (bf16[512,768]{1,0:T(8,128)(2,1)}, bf16[512,768]{1,0:T(8,128)(2,1)S(1)}, u32[]{:S(2)}) copy-start(bf16[512,768]{1,0:T(8,128)(2,1)S(1)} %fusion.15.own_ref.refs_1_.refs_0_) | copy-start | bytes 2359300
  200.3 30.3 %collective-permute-start.21 = (bf16[512,768]{1,0:T(8,128)(2,1)S(1)}, bf16[512,768]{1,0:T(8,128)(2,1)}, u32[]{:S(2)}, u32[]{:S(2)}) collective-permute-start(bf16[512,768]{1,0:T(8,128)(2,1)S(1)} %fusion.15.own_ref.refs_1_.refs_0_), channel_id=1, source_target_pairs={{0,1},{1,2},{2,3},{3,0},{4,5},{5,6},{6,7},{7,4},{8,9},{9,10},{10,1... | collective-permute-start | bytes 2359304 | tf_op jit(solution)/shard_map/ppermute | solution.py:220
  201.7 37.1 %collective-permute-start.22 = (bf16[512,768]{1,0:T(8,128)(2,1)S(1)}, bf16[512,768]{1,0:T(8,128)(2,1)}, u32[]{:S(2)}, u32[]{:S(2)}) collective-permute-start(bf16[512,768]{1,0:T(8,128)(2,1)S(1)} %fusion.15.own_ref.refs_1_.refs_0_), channel_id=1, source_target_pairs={{0,3},{1,0},{2,1},{3,2},{4,7},{5,4},{6,5},{7,6},{8,11},{9,8},{10,9... | collective-permute-start | bytes 2359304 | tf_op jit(solution)/shard_map/ppermute | solution.py:224
  207.7 21.1 %collective-permute-start.40 = (bf16[4,4,24,768]{3,2,1,0:T(8,128)(2,1)}, bf16[4,4,24,768]{3,2,1,0:T(8,128)(2,1)}, u32[]{:S(2)}, u32[]{:S(2)}) collective-permute-start(bf16[4,4,24,768]{3,2,1,0:T(8,128)(2,1)} %split.84), channel_id=1, source_target_pairs={{0,4},{4,0},{8,12},{12,8},{16,20},{20,16},{24,28},{28,24},{1,5},{5... | collective-permute-start | bytes 1769480 | tf_op jit(solution)/shard_map/ppermute | solution.py:185
  215.6 19.6 %collective-permute-start.33 = (bf16[4,2,72,768]{3,2,1,0:T(8,128)(2,1)}, bf16[4,2,72,768]{3,2,1,0:T(8,128)(2,1)}, u32[]{:S(2)}, u32[]{:S(2)}) collective-permute-start(bf16[4,2,72,768]{3,2,1,0:T(8,128)(2,1)} %split.75), channel_id=1, source_target_pairs={{0,4},{4,0},{8,12},{12,8},{16,20},{20,16},{24,28},{28,24},{1,5},{5... | collective-permute-start | bytes 2654216 | tf_op jit(solution)/shard_map/ppermute | solution.py:185
  215.9 14.7 %copy-start.14 = (bf16[8,4,24,768]{3,2,1,0:T(8,128)(2,1)S(1)}, bf16[8,4,24,768]{3,2,1,0:T(8,128)(2,1)}, u32[]{:S(2)}) copy-start(bf16[8,4,24,768]{3,2,1,0:T(8,128)(2,1)} %copy-done.13) | copy-start | bytes 3538948
  218.7 4.2 %collective-permute-start.25 = (f32[72,128]{1,0:T(8,128)}, f32[72,128]{1,0:T(8,128)S(1)}, u32[]{:S(2)}, u32[]{:S(2)}) collective-permute-start(f32[72,128]{1,0:T(8,128)} %after.16), channel_id=1, source_target_pairs={{0,16},{4,12},{8,24},{12,4},{16,0},{20,28},{24,8},{28,20},{1,17},{... | collective-permute-start | bytes 110600 | tf_op jit(solution)/shard_map/ppermute | solution.py:185
  223.6 4.9 %collective-permute-start.26 = (f32[72,128]{1,0:T(8,128)S(1)}, f32[72,128]{1,0:T(8,128)S(1)}, u32[]{:S(2)}, u32[]{:S(2)}) collective-permute-start(f32[72,128]{1,0:T(8,128)S(1)} %add.231), channel_id=1, source_target_pairs={{0,8},{4,20},{8,0},{12,28},{16,24},{20,4},{24,16},{28,12},{1,9},{5... | collective-permute-start | bytes 110600 | tf_op jit(solution)/shard_map/ppermute | solution.py:185
  226.6 8.8 %copy-start.7 = (bf16[8,2,72,768]{3,2,1,0:T(8,128)(2,1)S(1)}, bf16[8,2,72,768]{3,2,1,0:T(8,128)(2,1)}, u32[]{:S(2)}) copy-start(bf16[8,2,72,768]{3,2,1,0:T(8,128)(2,1)} %copy-done.6) | copy-start | bytes 5308420
  228.5 17.5 %collective-permute-start.20 = (bf16[256,768]{1,0:T(8,128)(2,1)S(1)}, bf16[256,768]{1,0:T(8,128)(2,1)S(1)}, u32[]{:S(2)}, u32[]{:S(2)}) collective-permute-start(bf16[256,768]{1,0:T(8,128)(2,1)S(1)} %slice.171), channel_id=1, source_target_pairs={{0,3},{1,0},{2,1},{3,2},{4,7},{5,4},{6,5},{7,6},{8,11},{9,8},{10,9... | collective-permute-start | bytes 1179656 | tf_op jit(solution)/shard_map/ppermute | solution.py:224
  228.8 31.8 %collective-permute-start.19 = (bf16[256,768]{1,0:T(8,128)(2,1)}, bf16[256,768]{1,0:T(8,128)(2,1)S(1)}, u32[]{:S(2)}, u32[]{:S(2)}) collective-permute-start(bf16[256,768]{1,0:T(8,128)(2,1)} %slice.170), channel_id=1, source_target_pairs={{0,1},{1,2},{2,3},{3,0},{4,5},{5,6},{6,7},{7,4},{8,9},{9,10},{10,1... | collective-permute-start | bytes 1179656 | tf_op jit(solution)/shard_map/ppermute | solution.py:220
  230.6 3.7 %collective-permute-start.27 = (f32[72,128]{1,0:T(8,128)S(1)}, f32[72,128]{1,0:T(8,128)S(1)}, u32[]{:S(2)}, u32[]{:S(2)}) collective-permute-start(f32[72,128]{1,0:T(8,128)S(1)} %add.232), channel_id=1, source_target_pairs={{0,4},{4,0},{8,12},{12,8},{16,20},{20,16},{24,28},{28,24},{1,5},{5... | collective-permute-start | bytes 110600 | tf_op jit(solution)/shard_map/ppermute | solution.py:185
  234.2 33.3 %collective-permute-start.41 = (bf16[2,4,24,768]{3,2,1,0:T(8,128)(2,1)}, bf16[2,4,24,768]{3,2,1,0:T(8,128)(2,1)}, u32[]{:S(2)}, u32[]{:S(2)}) collective-permute-start(bf16[2,4,24,768]{3,2,1,0:T(8,128)(2,1)} %get-tuple-element.60), channel_id=1, source_target_pairs={{0,8},{4,20},{8,0},{12,28},{16,24},{20,4},{24,16},{28,12},{1,9},{5... | collective-permute-start | bytes 884744 | tf_op jit(solution)/shard_map/ppermute | solution.py:185
  235.3 34.0 %collective-permute-start.23 = (bf16[256,768]{1,0:T(8,128)(2,1)}, bf16[256,768]{1,0:T(8,128)(2,1)S(1)}, u32[]{:S(2)}, u32[]{:S(2)}) collective-permute-start(bf16[256,768]{1,0:T(8,128)(2,1)} %slice.172), channel_id=1, source_target_pairs={{0,1},{1,2},{2,3},{3,0},{4,5},{5,6},{6,7},{7,4},{8,9},{9,10},{10,1... | collective-permute-start | bytes 1179656 | tf_op jit(solution)/shard_map/ppermute | solution.py:220
  238.8 36.4 %collective-permute-start.34 = (bf16[2,2,72,768]{3,2,1,0:T(8,128)(2,1)}, bf16[2,2,72,768]{3,2,1,0:T(8,128)(2,1)S(1)}, u32[]{:S(2)}, u32[]{:S(2)}) collective-permute-start(bf16[2,2,72,768]{3,2,1,0:T(8,128)(2,1)} %get-tuple-element.54), channel_id=1, source_target_pairs={{0,8},{4,20},{8,0},{12,28},{16,24},{20,4},{24,16},{28,12},{1,9},{5... | collective-permute-start | bytes 1327112 | tf_op jit(solution)/shard_map/ppermute | solution.py:185
  245.9 14.6 %copy-start.20 = (bf16[256,768]{1,0:T(8,128)(2,1)}, bf16[256,768]{1,0:T(8,128)(2,1)S(1)}, u32[]{:S(2)}) copy-start(bf16[256,768]{1,0:T(8,128)(2,1)S(1)} %collective-permute-done.20.second_ref.refs_2_) | copy-start | bytes 1179652
  245.9 27.2 %collective-permute-start.24 = (bf16[256,768]{1,0:T(8,128)(2,1)}, bf16[256,768]{1,0:T(8,128)(2,1)S(1)}, u32[]{:S(2)}, u32[]{:S(2)}) collective-permute-start(bf16[256,768]{1,0:T(8,128)(2,1)} %slice.173), channel_id=1, source_target_pairs={{0,3},{1,0},{2,1},{3,2},{4,7},{5,4},{6,5},{7,6},{8,11},{9,8},{10,9... | collective-permute-start | bytes 1179656 | tf_op jit(solution)/shard_map/ppermute | solution.py:224
  266.6 19.4 %collective-permute-start.28 = (bf16[2,96,768]{2,1,0:T(8,128)(2,1)S(1)}, bf16[2,96,768]{2,1,0:T(8,128)(2,1)S(1)}, u32[]{:S(2)}, u32[]{:S(2)}) collective-permute-start(bf16[2,96,768]{2,1,0:T(8,128)(2,1)S(1)} %get-tuple-element.61), channel_id=1, source_target_pairs={{0,2},{1,3},{2,0},{3,1},{4,6},{5,7},{6,4},{7,5},{8,10},{9,11},{10,... | collective-permute-start | bytes 884744 | tf_op jit(solution)/shard_map/ppermute | solution.py:193
  267.5 19.1 %collective-permute-start.29 = (bf16[2,96,768]{2,1,0:T(8,128)(2,1)S(1)}, bf16[2,96,768]{2,1,0:T(8,128)(2,1)}, u32[]{:S(2)}, u32[]{:S(2)}) collective-permute-start(bf16[2,96,768]{2,1,0:T(8,128)(2,1)S(1)} %get-tuple-element.63), channel_id=1, source_target_pairs={{0,1},{1,0},{2,3},{3,2},{4,5},{5,4},{6,7},{7,6},{8,9},{9,8},{10,11... | collective-permute-start | bytes 884744 | tf_op jit(solution)/shard_map/ppermute | solution.py:193
  269.2 22.3 %collective-permute-start.30 = (bf16[2,96,768]{2,1,0:T(8,128)(2,1)S(1)}, bf16[2,96,768]{2,1,0:T(8,128)(2,1)}, u32[]{:S(2)}, u32[]{:S(2)}) collective-permute-start(bf16[2,96,768]{2,1,0:T(8,128)(2,1)S(1)} %get-tuple-element.62), channel_id=1, source_target_pairs={{0,3},{1,2},{2,1},{3,0},{4,7},{5,6},{6,5},{7,4},{8,11},{9,10},{10,... | collective-permute-start | bytes 884744 | tf_op jit(solution)/shard_map/ppermute | solution.py:193
  273.2 22.4 %collective-permute-start.42 = (bf16[1,4,24,768]{3,2,1,0:T(8,128)(2,1)S(1)}, bf16[1,4,24,768]{3,2,1,0:T(8,128)(2,1)S(1)}, u32[]{:S(2)}, u32[]{:S(2)}) collective-permute-start(bf16[1,4,24,768]{3,2,1,0:T(8,128)(2,1)S(1)} %add_convert_fusion.8), channel_id=1, source_target_pairs={{0,16},{4,12},{8,24},{12,4},{16,0},{20,28},{24,8},{28,20},{1,17},{... | collective-permute-start | bytes 442376 | tf_op jit(solution)/shard_map/ppermute | solution.py:185
  275.3 31.1 %collective-permute-start.35 = (bf16[1,2,72,768]{3,2,1,0:T(8,128)(2,1)S(1)}, bf16[1,2,72,768]{3,2,1,0:T(8,128)(2,1)S(1)}, u32[]{:S(2)}, u32[]{:S(2)}) collective-permute-start(bf16[1,2,72,768]{3,2,1,0:T(8,128)(2,1)S(1)} %add_convert_fusion.5), channel_id=1, source_target_pairs={{0,16},{4,12},{8,24},{12,4},{16,0},{20,28},{24,8},{28,20},{1,17},{... | collective-permute-start | bytes 663560 | tf_op jit(solution)/shard_map/ppermute | solution.py:185
  293.7 14.0 %collective-permute-start.49 = (bf16[2,1,96,768]{3,2,1,0:T(8,128)(2,1)}, bf16[2,1,96,768]{3,2,1,0:T(8,128)(2,1)S(1)}, u32[]{:S(2)}, u32[]{:S(2)}) collective-permute-start(bf16[2,1,96,768]{3,2,1,0:T(8,128)(2,1)} %fusion.27.refs_1_), channel_id=1, source_target_pairs={{0,16},{4,12},{8,24},{12,4},{16,0},{20,28},{24,8},{28,20},{1,17},{... | collective-permute-start | bytes 884744 | tf_op jit(solution)/shard_map/ppermute | solution.py:185
  297.3 15.4 %collective-permute-start.43 = (bf16[24,768]{1,0:T(8,128)(2,1)S(1)}, bf16[24,768]{1,0:T(8,128)(2,1)S(1)}, u32[]{:S(2)}, u32[]{:S(2)}) collective-permute-start(bf16[24,768]{1,0:T(8,128)(2,1)S(1)} %get-tuple-element.70), channel_id=1, source_target_pairs={{0,2},{1,3},{2,0},{3,1},{4,6},{5,7},{6,4},{7,5},{8,10},{9,11},{10,... | collective-permute-start | bytes 110600 | tf_op jit(solution)/shard_map/ppermute | solution.py:193
  303.0 9.8 %collective-permute-start.44 = (bf16[24,768]{1,0:T(8,128)(2,1)S(1)}, bf16[24,768]{1,0:T(8,128)(2,1)S(1)}, u32[]{:S(2)}, u32[]{:S(2)}) collective-permute-start(bf16[24,768]{1,0:T(8,128)(2,1)S(1)} %get-tuple-element.72), channel_id=1, source_target_pairs={{0,1},{1,0},{2,3},{3,2},{4,5},{5,4},{6,7},{7,6},{8,9},{9,8},{10,11... | collective-permute-start | bytes 110600 | tf_op jit(solution)/shard_map/ppermute | solution.py:193
  304.2 8.6 %collective-permute-start.45 = (bf16[24,768]{1,0:T(8,128)(2,1)S(1)}, bf16[24,768]{1,0:T(8,128)(2,1)S(1)}, u32[]{:S(2)}, u32[]{:S(2)}) collective-permute-start(bf16[24,768]{1,0:T(8,128)(2,1)S(1)} %get-tuple-element.71), channel_id=1, source_target_pairs={{0,3},{1,2},{2,1},{3,0},{4,7},{5,6},{6,5},{7,4},{8,11},{9,10},{10,... | collective-permute-start | bytes 110600 | tf_op jit(solution)/shard_map/ppermute | solution.py:193
  306.5 4.6 %collective-permute-start.31 = (f32[72,128]{1,0:T(8,128)}, f32[72,128]{1,0:T(8,128)S(1)}, u32[]{:S(2)}, u32[]{:S(2)}) collective-permute-start(f32[72,128]{1,0:T(8,128)} %after.18), channel_id=1, source_target_pairs={{0,1},{1,0},{2,3},{3,2},{4,5},{5,4},{6,7},{7,6},{8,9},{9,8},{10,11... | collective-permute-start | bytes 110600 | tf_op jit(solution)/shard_map/ppermute | solution.py:193
  308.7 10.3 %collective-permute-start.50 = (bf16[2,2,96,768]{3,2,1,0:T(8,128)(2,1)S(1)}, bf16[2,2,96,768]{3,2,1,0:T(8,128)(2,1)S(1)}, u32[]{:S(2)}, u32[]{:S(2)}) collective-permute-start(bf16[2,2,96,768]{3,2,1,0:T(8,128)(2,1)S(1)} %pad_maximum_fusion.9), channel_id=1, source_target_pairs={{0,8},{4,20},{8,0},{12,28},{16,24},{20,4},{24,16},{28,12},{1,9},{5... | collective-permute-start | bytes 1769480 | tf_op jit(solution)/shard_map/ppermute | solution.py:185
  311.1 9.1 %collective-permute-start.36 = (bf16[72,768]{1,0:T(8,128)(2,1)S(1)}, bf16[72,768]{1,0:T(8,128)(2,1)S(1)}, u32[]{:S(2)}, u32[]{:S(2)}) collective-permute-start(bf16[72,768]{1,0:T(8,128)(2,1)S(1)} %slice_bitcast_fusion), channel_id=1, source_target_pairs={{0,2},{1,3},{2,0},{3,1},{4,6},{5,7},{6,4},{7,5},{8,10},{9,11},{10,... | collective-permute-start | bytes 331784 | tf_op jit(solution)/shard_map/ppermute | solution.py:193
  312.8 7.6 %collective-permute-start.46 = (bf16[1,24,768]{2,1,0:T(8,128)(2,1)S(1)}, bf16[1,24,768]{2,1,0:T(8,128)(2,1)S(1)}, u32[]{:S(2)}, u32[]{:S(2)}) collective-permute-start(bf16[1,24,768]{2,1,0:T(8,128)(2,1)S(1)} %fusion.33), channel_id=1, source_target_pairs={{0,16},{4,12},{8,24},{12,4},{16,0},{20,28},{24,8},{28,20},{1,17},{... | collective-permute-start | bytes 110600 | tf_op jit(solution)/shard_map/ppermute | solution.py:185
  313.5 8.8 %copy-start.40 = (f32[72,128]{1,0:T(8,128)S(1)}, f32[72,128]{1,0:T(8,128)}, u32[]{:S(2)}) copy-start(f32[72,128]{1,0:T(8,128)} %after.19) | copy-start | bytes 110596
  313.5 8.8 %collective-permute-start.32 = (f32[72,128]{1,0:T(8,128)}, f32[72,128]{1,0:T(8,128)S(1)}, u32[]{:S(2)}, u32[]{:S(2)}) collective-permute-start(f32[72,128]{1,0:T(8,128)} %after.19), channel_id=1, source_target_pairs={{0,2},{1,3},{2,0},{3,1},{4,6},{5,7},{6,4},{7,5},{8,10},{9,11},{10,... | collective-permute-start | bytes 110600 | tf_op jit(solution)/shard_map/ppermute | solution.py:193
  320.1 16.5 %collective-permute-start.51 = (bf16[2,4,96,768]{3,2,1,0:T(8,128)(2,1)S(1)}, bf16[2,4,96,768]{3,2,1,0:T(8,128)(2,1)S(1)}, u32[]{:S(2)}, u32[]{:S(2)}) collective-permute-start(bf16[2,4,96,768]{3,2,1,0:T(8,128)(2,1)S(1)} %pad_maximum_fusion.4), channel_id=1, source_target_pairs={{0,4},{4,0},{8,12},{12,8},{16,20},{20,16},{24,28},{28,24},{1,5},{5... | collective-permute-start | bytes 3538952 | tf_op jit(solution)/shard_map/ppermute | solution.py:185
  320.2 5.5 %collective-permute-start.37 = (bf16[1,72,768]{2,1,0:T(8,128)(2,1)S(1)}, bf16[1,72,768]{2,1,0:T(8,128)(2,1)S(1)}, u32[]{:S(2)}, u32[]{:S(2)}) collective-permute-start(bf16[1,72,768]{2,1,0:T(8,128)(2,1)S(1)} %fusion.29), channel_id=1, source_target_pairs={{0,16},{4,12},{8,24},{12,4},{16,0},{20,28},{24,8},{28,20},{1,17},{... | collective-permute-start | bytes 331784 | tf_op jit(solution)/shard_map/ppermute | solution.py:185
  320.4 11.4 %collective-permute-start.47 = (bf16[2,24,768]{2,1,0:T(8,128)(2,1)S(1)}, bf16[2,24,768]{2,1,0:T(8,128)(2,1)S(1)}, u32[]{:S(2)}, u32[]{:S(2)}) collective-permute-start(bf16[2,24,768]{2,1,0:T(8,128)(2,1)S(1)} %pad_maximum_fusion.18), channel_id=1, source_target_pairs={{0,8},{4,20},{8,0},{12,28},{16,24},{20,4},{24,16},{28,12},{1,9},{5... | collective-permute-start | bytes 221192 | tf_op jit(solution)/shard_map/ppermute | solution.py:185
  325.7 6.0 %collective-permute-start.38 = (bf16[2,72,768]{2,1,0:T(8,128)(2,1)S(1)}, bf16[2,72,768]{2,1,0:T(8,128)(2,1)S(1)}, u32[]{:S(2)}, u32[]{:S(2)}) collective-permute-start(bf16[2,72,768]{2,1,0:T(8,128)(2,1)S(1)} %pad_maximum_fusion.16), channel_id=1, source_target_pairs={{0,8},{4,20},{8,0},{12,28},{16,24},{20,4},{24,16},{28,12},{1,9},{5... | collective-permute-start | bytes 663560 | tf_op jit(solution)/shard_map/ppermute | solution.py:185
  331.8 4.7 %collective-permute-start.39 = (bf16[4,72,768]{2,1,0:T(8,128)(2,1)S(1)}, bf16[4,72,768]{2,1,0:T(8,128)(2,1)S(1)}, u32[]{:S(2)}, u32[]{:S(2)}) collective-permute-start(bf16[4,72,768]{2,1,0:T(8,128)(2,1)S(1)} %pad_maximum_fusion.11), channel_id=1, source_target_pairs={{0,4},{4,0},{8,12},{12,8},{16,20},{20,16},{24,28},{28,24},{1,5},{5... | collective-permute-start | bytes 1327112 | tf_op jit(solution)/shard_map/ppermute | solution.py:185
  331.9 2.0 collective-permute-start.48
  (49 other events, 132.2 us)
Sparse Core Ops, SparseCore 0:
  11.7 91.2 all-gather.1
  130.5 75.3 reduce-scatter.1
